TPU v7x, 512 devices: a whole 4x4x16 slice. The times are simulated.
512 devices in a mesh: dom: 128 (over y, z, core), feat: 4 (over x).
Axes of the slice: x: 4, y: 4, z: 16, core: 2. Of those that a mesh axis runs over, the one named last changes fastest.
Arguments:
- node_feats: bfloat16 [131072, 512], P('dom', 'feat'), may hold values from -6 to 6
- neigh_weight: bfloat16 [1024, 512], P(None, 'feat'), may hold values from -0.25 to 0.25
- bias: float32 [512], P('feat'), may hold values from -3 to 3
- out_grad: bfloat16 [131072, 512], P('dom', 'feat'), may hold values from -6 to 6
- tile_values: bfloat16 [11264, 128, 128], P('dom'), may hold values from 0 to 1, as said below
- tile_src: int32 [11264], P('dom'), may hold values from 0 to 43, as said below
- tile_dst: int32 [11264], P('dom'), may hold values from 0 to 7
- tile_count: int32 [128], P('dom'), may hold values from 22 to 88, as said below
- hub_rows: int32 [4096], P('dom'), may hold values from 0 to 1023
- send_rows: int32 [16384, 4], P('dom'), may hold values from 0 to 1023
Outputs:
- layer_out: bfloat16 [131072, 512], P('dom', 'feat')
- node_grad: bfloat16 [131072, 512], P('dom', 'feat')
- weight_grad: float32 [1024, 512], P(None, 'feat')
- bias_grad: float32 [512], P('feat')
Inputs may be any that keep to these rules, and one draw needn't show every extreme that they name: `tile_src`: in each partition tile t < 8 has source and destination block t, and the next 4 tiles have the halo blocks as sources in order; later tiles have any source block. `tile_count`: some partition has all 88 tiles live in every draw. `tile_values`: entries are 0 or 1; slots past a partition's live count hold arbitrary 0/1 entries.
All inputs are finite; a program needn't handle non-finite values.
Results may differ from a plain program's by a relative error of at most 0.007.
Values may be sent and summed in bfloat16 or wider, within the bound.
A program may use at most 64 MiB of HBM per device.

v0:
```python
import math

import jax
import jax.numpy as jnp
from jax import lax
from jax.sharding import PartitionSpec as P

HIGHEST_PREC = lax.Precision.HIGHEST


def silu_slope(pre_act):
    sigmoid_val = jax.nn.sigmoid(pre_act)
    return sigmoid_val * (1.0 + pre_act * (1.0 - sigmoid_val))


def per_device(
    node_feats,
    neigh_weight,
    bias,
    out_grad,
    tile_values,
    tile_src,
    tile_dst,
    tile_count,
    hub_rows,
    send_rows,
):
    node_rows, col_width = node_feats.shape
    tile_total, tile_side = (tile_values.shape[0], tile_values.shape[1])
    peer_count = lax.axis_size("dom")
    cut_rows = send_rows.shape[1]
    hub_owned = hub_rows.shape[0]
    halo_rows = peer_count * cut_rows
    src_blocks = (node_rows + halo_rows + hub_owned * peer_count) // tile_side
    dst_blocks = node_rows // tile_side
    model_width = neigh_weight.shape[0] // 2
    live_tiles = (jnp.arange(tile_total) < tile_count[0]).astype(jnp.float32)
    dst_hot = (tile_dst[:, None] == jnp.arange(dst_blocks)[None, :]).astype(
        jnp.float32
    ) * live_tiles[:, None]
    src_hot = (tile_src[:, None] == jnp.arange(src_blocks)[None, :]).astype(
        jnp.float32
    ) * live_tiles[:, None]
    outgoing = node_feats[send_rows]
    halo_feats = lax.all_to_all(outgoing, "dom", split_axis=0, concat_axis=0, tiled=True).reshape(
        halo_rows, col_width
    )
    hub_table = lax.all_gather(node_feats[hub_rows], "dom", axis=0, tiled=True)
    row_totals = jnp.sum(tile_values, axis=2, dtype=jnp.float32)
    degree = jnp.einsum("tn,ti->ni", dst_hot, row_totals, precision=HIGHEST_PREC).reshape(node_rows)
    inverse = 1.0 / jnp.maximum(degree, 1.0)
    source_rows = jnp.concatenate([node_feats, halo_feats, hub_table], axis=0)
    picked = source_rows.reshape(src_blocks, tile_side, col_width)[tile_src]
    products = jnp.einsum("tij,tjf->tif", tile_values, picked, preferred_element_type=jnp.float32)
    row_sums = jnp.einsum("tn,tif->nif", dst_hot, products, precision=HIGHEST_PREC).reshape(
        node_rows, col_width
    )
    neigh_mean = (row_sums * inverse[:, None]).astype(jnp.bfloat16)
    full_self, full_mean = (
        lax.all_gather(node_feats, "feat", axis=1, tiled=True),
        lax.all_gather(neigh_mean, "feat", axis=1, tiled=True),
    )
    pre_act = jnp.dot(full_self, neigh_weight[:model_width], preferred_element_type=jnp.float32)
    pre_act = (
        pre_act
        + jnp.dot(full_mean, neigh_weight[model_width:], preferred_element_type=jnp.float32)
        + bias
    )
    layer_out = jax.nn.silu(pre_act).astype(jnp.bfloat16)
    grad_pre = (out_grad.astype(jnp.float32) * silu_slope(pre_act)).astype(jnp.bfloat16)
    contract = (((0,), (0,)), ((), ()))
    local_weight = jnp.concatenate(
        [
            lax.dot_general(full_self, grad_pre, contract, preferred_element_type=jnp.float32),
            lax.dot_general(full_mean, grad_pre, contract, preferred_element_type=jnp.float32),
        ],
        axis=0,
    )
    local_bias = jnp.sum(grad_pre, axis=0, dtype=jnp.float32)
    weight_sum, bias_sum = lax.psum((local_weight, local_bias), "dom")
    grad_scale = 1.0 / math.sqrt(node_rows * peer_count)
    weight_grad = weight_sum * grad_scale
    bias_grad = bias_sum * grad_scale
    self_rows, mean_rows = (
        lax.all_to_all(neigh_weight[:model_width], "feat", split_axis=0, concat_axis=1, tiled=True),
        lax.all_to_all(neigh_weight[model_width:], "feat", split_axis=0, concat_axis=1, tiled=True),
    )
    weight_full = jnp.concatenate([self_rows, mean_rows], axis=0)
    grad_cat = lax.dot_general(
        lax.all_gather(grad_pre, "feat", axis=1, tiled=True),
        weight_full,
        (((1,), (1,)), ((), ())),
        preferred_element_type=jnp.float32,
    )
    grad_self = grad_cat[:, :col_width]
    grad_mean = (grad_cat[:, col_width:] * inverse[:, None]).astype(jnp.bfloat16)
    chosen = grad_mean.reshape(dst_blocks, tile_side, col_width)[tile_dst]
    back_terms = jnp.einsum("tij,tif->tjf", tile_values, chosen, preferred_element_type=jnp.float32)
    spread = jnp.einsum("ts,tjf->sjf", src_hot, back_terms, precision=HIGHEST_PREC).reshape(
        src_blocks * tile_side, col_width
    )
    halo_grad = (
        spread[node_rows : node_rows + halo_rows]
        .astype(jnp.bfloat16)
        .reshape(peer_count, cut_rows, col_width)
    )
    hub_grad = spread[node_rows + halo_rows :]
    returned = lax.all_to_all(halo_grad, "dom", split_axis=0, concat_axis=0, tiled=True)
    hub_mine = lax.psum_scatter(hub_grad, "dom", scatter_dimension=0, tiled=True)
    grad_total = grad_self + spread[:node_rows]
    grad_total = grad_total.at[send_rows.reshape(halo_rows)].add(
        returned.reshape(halo_rows, col_width).astype(jnp.float32)
    )
    grad_total = grad_total.at[hub_rows].add(hub_mine)
    return (layer_out, grad_total.astype(jnp.bfloat16), weight_grad, bias_grad)


def solution(mesh):
    in_specs = (
        P("dom", "feat"),
        P(None, "feat"),
        P("feat"),
        P("dom", "feat"),
        P("dom", None, None),
        P("dom"),
        P("dom"),
        P("dom"),
        P("dom"),
        P("dom", None),
    )
    out_specs = (P("dom", "feat"), P("dom", "feat"), P(None, "feat"), P("feat"))
    return jax.shard_map(
        per_device, mesh=mesh, in_specs=in_specs, out_specs=out_specs, check_vma=False
    )
```

profile of v0, /device:TPU:1, one launch (start us, length us, event | category | flops | bytes accessed | tf_op | source)
XLA Modules:
  0.0 851.6 jit_solution(6210575488350903997)
XLA Ops:
  7.2 0.7 compare_select_fusion.4
  7.9 2.2 gather_fusion.1
  10.1 0.0 all-gather.6.cloned.1.call-start
  10.2 0.7 all-gather.6.cloned.1.call-update
  10.9 0.7 compare_select_fusion.1
  11.6 0.1 copy.38
  11.7 0.1 reshape.94
  11.8 2.7 gather_fusion
  14.4 20.6 %all-to-all-start = ((bf16[128,4,128]{2,1,0:T(4,128)(2,1)}), bf16[128,4,128]{2,1,0:T(4,128)(2,1)S(1)}, u32[]{:S(2)}, u32[]{:S(2)}) async-start(bf16[128,4,128]{2,1,0:T(4,128)(2,1)} %bitcast.2), calls=%async_computation | async-start | bytes 262144 | tf_op jit(solution)/shard_map/all_to_all | solution.py:45
  35.0 0.0 all-gather.8.cloned.1.call-start
  35.7 0.7 compare_select_fusion.3
  36.4 2.6 convert_reduce_fusion
  39.0 0.1 fusion.2
  39.2 13.2 %all-to-all-done = bf16[128,4,128]{2,1,0:T(4,128)(2,1)S(1)} async-done(((bf16[128,4,128]{2,1,0:T(4,128)(2,1)}), bf16[128,4,128]{2,1,0:T(4,128)(2,1)S(1)}, u32[]{:S(2)}, u32[]{:S(2)}) %all-to-all-start) | async-done | bytes 131104 | tf_op jit(solution)/shard_map/all_to_all | solution.py:45
  52.4 96.0 %all-gather.12.cloned.1.call-done = bf16[4096,128]{1,0:T(8,128)(2,1)} async-done(((bf16[32,128]{1,0:T(8,128)(2,1)}), bf16[4096,128]{1,0:T(8,128)(2,1)}) %all-gather.12.cloned.1.call-update) | async-done | bytes 1048592 | tf_op jit(solution)/shard_map/all_gather | solution.py:48
  148.4 2.4 pad_maximum_fusion
  150.9 4.2 gather_fusion.2
  155.1 6.5 convolution_bitcast_fusion.1
  161.5 6.6 copy.40
  168.1 4.9 fusion.18
  173.0 0.1 copy.41
  173.1 0.9 fusion.4
  174.0 0.0 all-gather.10.cloned.1.call-start
  174.1 4.3 all-gather.6.cloned.1.call-done
  178.4 2.4 fusion.30
  180.9 34.8 %all-gather.8.cloned.1.call-done = bf16[1024,512]{1,0:T(8,128)(2,1)} async-done(((bf16[1024,128]{1,0:T(8,128)(2,1)}), bf16[1024,512]{1,0:T(8,128)(2,1)}) %all-gather.8.cloned.1.call-update) | async-done | bytes 1048592 | tf_op jit(solution)/shard_map/all_gather | solution.py:61
  215.7 3.1 convert_reduce_fusion.1
  218.9 0.7 fusion.32
  219.6 3.7 all-to-all-start.2
  223.3 4.8 all-to-all-done.2
  228.1 3.3 all-to-all-start.1
  231.5 0.0 all-reduce.2.cloned.1.call-start
  231.5 0.1 copy.43
  231.7 4.6 all-to-all-done.1
  236.2 0.1 copy.42
  236.4 1.6 fusion.33
  238.0 1.6 convolution_bitcast_fusion.2
  239.6 0.8 pad_maximum_fusion.1
  240.5 0.2 reduce-scatter.2.cloned.1.call-start
  240.7 12.9 %all-gather.10.cloned.1.call-done = bf16[1024,512]{1,0:T(8,128)(2,1)} async-done(((bf16[1024,128]{1,0:T(8,128)(2,1)}), bf16[1024,512]{1,0:T(8,128)(2,1)}) %all-gather.10.cloned.1.call-update) | async-done | bytes 1048592 | tf_op jit(solution)/shard_map/all_gather | solution.py:90
  253.6 1.7 fusion.5
  255.3 1.0 copy-done.2
  256.3 0.2 fusion.3
  256.5 2.7 gather_fusion.3
  259.2 5.4 convolution_bitcast_fusion
  264.6 6.5 copy.45
  271.1 5.0 fusion.11
  276.1 0.3 slice.52
  276.4 2.6 copy.49
  279.0 0.1 copy.47
  279.1 0.1 reshape.90
  279.3 249.1 %psum.15 = f32[128]{0:T(128)S(1)} all-reduce(f32[128]{0:T(128)S(1)} %copy-done.10), channel_id=1, replica_groups=mesh['dom'=128,'feat'=4] {'dom'}, use_global_device_ids=true, to_apply=%region_6.7 | all-reduce | flops 128 | bytes 1024 | tf_op jit(solution)/shard_map/psum | solution.py:80
  528.4 0.7 copy.48
  529.0 9.3 %all-to-all-start.3 = ((bf16[128,4,128]{2,1,0:T(4,128)(2,1)}), bf16[128,4,128]{2,1,0:T(4,128)(2,1)S(1)}, u32[]{:S(2)}, u32[]{:S(2)}) async-start(bf16[128,4,128]{2,1,0:T(4,128)(2,1)} %bitcast.19), calls=%async_computation.3 | async-start | bytes 262144 | tf_op jit(solution)/shard_map/all_to_all | solution.py:108
  538.3 0.5 broadcast_multiply_fusion.1
  538.8 51.5 %all-reduce.2.cloned.1.call-done = f32[1024,128]{0,1:T(8,128)} async-done(((f32[1024,128]{0,1:T(8,128)}), f32[1024,128]{0,1:T(8,128)}) %all-reduce.2.cloned.1.call-update) | async-done | bytes 524304 | tf_op jit(solution)/shard_map/psum | solution.py:80
  590.3 1.9 broadcast_multiply_fusion
  592.2 2.0 copy.51
  594.3 0.1 copy.46
  594.4 1.1 slice_add_fusion
  595.5 3.5 scatter_custom_fusion
  599.0 243.9 %reduce-scatter.2.cloned.1.call-done = f32[32,128]{1,0:T(8,128)} async-done(((f32[4096,128]{1,0:T(8,128)}), f32[32,128]{1,0:T(8,128)}) %reduce-scatter.2.cloned.1.call-update) | async-done | bytes 16400 | tf_op jit(solution)/shard_map/reduce_scatter | solution.py:109
  842.9 1.1 scatter_fusion
  844.0 0.7 convert_element_type.54
  (37 shorter events, 0.3 us)
Async XLA Ops:
  7.2 141.3 %copy-start.1 = (bf16[1024,128]{1,0:T(8,128)(2,1)S(1)}, bf16[1024,128]{1,0:T(8,128)(2,1)}, u32[]{:S(2)}) copy-start(bf16[1024,128]{1,0:T(8,128)(2,1)} %param.10) | copy-start | bytes 786436
  7.2 31.9 %copy-start.6 = (s32[88]{0:T(128)S(1)}, s32[88]{0:T(128)}, u32[]{:S(2)}) copy-start(s32[88]{0:T(128)} %param.16) | copy-start | bytes 1060
  7.2 141.3 %all-gather.12.cloned.1.call-start = ((), (), s32[]{:S(2)}) async-start(), calls=%async_computation.10 | async-start | bytes 1056768 | tf_op jit(solution)/shard_map/all_gather | solution.py:48
  10.1 168.3 %all-gather.6.cloned.1.call-start = ((), (), s32[]{:S(2)}) async-start(), calls=%async_computation.5 | async-start | bytes 1310720 | tf_op jit(solution)/shard_map/all_gather | solution.py:60
  14.4 38.0 %all-to-all-start = ((bf16[128,4,128]{2,1,0:T(4,128)(2,1)}), bf16[128,4,128]{2,1,0:T(4,128)(2,1)S(1)}, u32[]{:S(2)}, u32[]{:S(2)}) async-start(bf16[128,4,128]{2,1,0:T(4,128)(2,1)} %bitcast.2), calls=%async_computation | async-start | bytes 262144 | tf_op jit(solution)/shard_map/all_to_all | solution.py:45
  35.0 180.7 %all-gather.8.cloned.1.call-start = ((), (), s32[]{:S(2)}) async-start(), calls=%async_computation.6 | async-start | bytes 1310720 | tf_op jit(solution)/shard_map/all_gather | solution.py:61
  150.9 4.2 copy-start
  168.1 10.3 %copy-start.4 = (bf16[1024,128]{1,0:T(8,128)(2,1)S(1)}, bf16[1024,128]{1,0:T(8,128)(2,1)}, u32[]{:S(2)}) copy-start(bf16[1024,128]{1,0:T(8,128)(2,1)} %param.11) | copy-start | bytes 786436
  173.0 42.8 %copy-start.8 = (bf16[1024,128]{1,0:T(8,128)(2,1)S(1)}, bf16[1024,128]{1,0:T(8,128)(2,1)}, u32[]{:S(2)}) copy-start(bf16[1024,128]{1,0:T(8,128)(2,1)} %param.13) | copy-start | bytes 786436
  173.0 42.7 %copy-start.9 = (f32[128]{0:T(128)S(1)}, f32[128]{0:T(128)}, u32[]{:S(2)}) copy-start(f32[128]{0:T(128)} %param.12) | copy-start | bytes 1540
  174.0 79.6 %all-gather.10.cloned.1.call-start = ((), (), s32[]{:S(2)}) async-start(), calls=%async_computation.7 | async-start | bytes 1310720 | tf_op jit(solution)/shard_map/all_gather | solution.py:90
  218.9 19.2 %copy-start.3 = (bf16[1024,128]{1,0:T(8,128)(2,1)S(1)}, bf16[1024,128]{1,0:T(8,128)(2,1)}, u32[]{:S(2)}) copy-start(bf16[1024,128]{1,0:T(8,128)(2,1)} %get-tuple-element.21) | copy-start | bytes 786436
  219.6 8.5 %all-to-all-start.2 = ((bf16[4,128,128]{2,1,0:T(8,128)(2,1)}), bf16[4,128,128]{2,1,0:T(8,128)(2,1)S(1)}, u32[]{:S(2)}, u32[]{:S(2)}) async-start(bf16[4,128,128]{2,1,0:T(8,128)(2,1)} %bitcast.11), calls=%async_computation.2 | async-start | bytes 262144 | tf_op jit(solution)/shard_map/all_to_all | solution.py:86
  228.1 8.1 all-to-all-start.1
  231.5 358.8 %all-reduce.2.cloned.1.call-start = ((), (), s32[]{:S(2)}) async-start(), calls=%async_computation.9 | async-start | bytes 1048576 | tf_op jit(solution)/shard_map/psum | solution.py:80
  240.5 602.4 %reduce-scatter.2.cloned.1.call-start = ((), (), s32[]{:S(2)}) async-start(), calls=%async_computation.8 | async-start | bytes 2113536 | tf_op jit(solution)/shard_map/reduce_scatter | solution.py:109
  255.3 1.0 copy-start.2
  264.6 6.5 copy-start.7
  276.4 2.6 copy-start.5
  276.4 2.8 copy-start.10
  529.0 66.4 %all-to-all-start.3 = ((bf16[128,4,128]{2,1,0:T(4,128)(2,1)}), bf16[128,4,128]{2,1,0:T(4,128)(2,1)S(1)}, u32[]{:S(2)}, u32[]{:S(2)}) async-start(bf16[128,4,128]{2,1,0:T(4,128)(2,1)} %bitcast.19), calls=%async_computation.3 | async-start | bytes 262144 | tf_op jit(solution)/shard_map/all_to_all | solution.py:108
Sparse Core Ops, SparseCore 0:
  11.6 136.8 all-gather.11
  150.5 27.8 all-gather.5
  181.1 34.5 all-gather.7
  219.0 34.5 all-gather.9
  257.5 332.7 all-reduce.1
  595.4 247.4 reduce-scatter.1
where the time goes:
time: 863 us; the launch traced here: 852 us
  waiting for transfers between devices  467 us (54%)
  blocking collectives  249 us (29%)
  starting transfers between devices  37.3 us (4%)
  local copies, waits for them, and re-layouts  33.1 us (4%)
  matrix products  32.3 us (4%)
  other arithmetic  18 us (2%)
  between operations  15 us (2%)
    psum x1, blocking collectives, per_device(): weight_sum, bias_sum = lax.psum((local_weight, local_bias), 'dom')  249 us
    reduce_scatter x1, waiting for transfers between devices, per_device(): lax.psum_scatter(hub_grad, 'dom', scatter_dimension=0, tiled=True)  244 us
    all_gather x1, waiting for transfers between devices, per_device(): hub_table = lax.all_gather(node_feats[hub_rows], 'dom', axis=0, tiled=True)  96 us
    psum x1, waiting for transfers between devices, per_device(): weight_sum, bias_sum = lax.psum((local_weight, local_bias), 'dom')  51.5 us
    all_gather x1, waiting for transfers between devices, per_device(): lax.all_gather(neigh_mean, 'feat', axis=1, tiled=True)  34.8 us
    all_to_all x1, starting transfers between devices, per_device(): lax.all_to_all(outgoing, 'dom', split_axis=0, concat_axis=0, tiled=True)  20.6 us
  transfers between devices with their start and end apart: 10, of which 9 were waited for; matrix products, arithmetic and copies ran while one was open for 9% of the time, Pallas kernels for 0%

commit v1 on v0

v1 whole, which is shorter than its diff:
```python
import functools
import math

import jax
import jax.numpy as jnp
from jax import lax
from jax.experimental import pallas as pl
from jax.experimental.pallas import tpu as pltpu
from jax.sharding import PartitionSpec as P

BF16 = jnp.bfloat16
F32 = jnp.float32
CORES = 2
Y_CHIPS = 4


def dot(a, b):
    return jnp.dot(a, b, preferred_element_type=F32)


def dot_nt(a, b):
    return lax.dot_general(a, b, (((1,), (1,)), ((), ())), preferred_element_type=F32)


def dot_tn(a, b):
    return lax.dot_general(a, b, (((0,), (0,)), ((), ())), preferred_element_type=F32)


class Group:
    def __init__(self, size, me, device):
        self.size, self.me, self.device = size, me, device

    def each(self, body):
        if self.size <= 4:
            for step in range(1, self.size):
                body(step, lax.rem(self.me + step, self.size))
        else:

            def loop(step, carry):
                body(step, lax.rem(self.me + step, self.size))
                return carry

            lax.fori_loop(1, self.size, loop, 0)


class Exchange:
    def __init__(self, group, src, dst, sems):
        self.group, self.src, self.dst, self.sems = group, src, dst, sems

    def copy(self, step, peer, landing):
        return pltpu.make_async_remote_copy(
            src_ref=self.src(peer),
            dst_ref=self.dst(landing),
            send_sem=self.sems.at[0, step],
            recv_sem=self.sems.at[1, landing],
            device_id=self.group.device(peer),
            device_id_type=pl.DeviceIdType.MESH,
        )

    def start_one(self, step, peer):
        self.copy(step, peer, self.group.me).start()

    def start(self):
        self.group.each(self.start_one)

    def wait_one(self, step, peer):
        self.copy(step, peer, peer).wait_recv()

    def wait(self):
        self.group.each(self.wait_one)

    def drain(self):
        self.group.each(lambda step, peer: self.copy(step, peer, self.group.me).wait_send())


def kernel(
    dims,
    nf,
    weight,
    bias,
    out_grad,
    tiles,
    idx_col,
    idx_row,
    prev,
    last,
    layer_out,
    node_grad,
    weight_grad,
    bias_grad,
    tile_buf,
    acc_tiles,
    acc_tiles_t,
    adj,
    adj_t,
    out_halo,
    st1,
    st2,
    halo_z,
    halo,
    hub,
    deg,
    acc,
    selfc,
    meanc,
    ogc,
    wfull,
    biasc,
    mean,
    pre,
    lo_send,
    lo_recv,
    gp,
    gm_send,
    gm,
    gs_send,
    gs_recv,
    wg32,
    wgb,
    wg_core,
    wx_send,
    wx_recv,
    wx_own,
    wy_send,
    wy_recv,
    wy_own,
    wz_send,
    wz_recv,
    wout,
    bias_core,
    hs32,
    hsb,
    hs_core,
    hy_send,
    hy_recv,
    hy_own,
    hz_send,
    hz_recv,
    halo_b,
    halo_zb,
    rt1,
    halo_m,
    rt2,
    total,
    tile_sem,
    s_yc,
    s_z,
    s_hz,
    s_hy,
    s_hc,
    s_xs,
    s_xo,
    s_xw,
    s_xb,
    s_wc,
    s_xm,
    s_xl,
    s_xg,
    s_xgs,
    s_gc,
    s_gx,
    s_gy,
    s_gz,
    s_az,
    s_ay,
    s_ac,
    s_bc,
    s_bhc,
    s_bhy,
    s_bhz,
    s_rz,
    s_ryc,
):
    Y, Z, C, X, N, T, NT, F, HD, CUT, scale = dims
    D = X * F
    R = N // X
    HALO = Y * Z * C * CUT
    NB = N // T
    SB = (N + HALO + Y * Z * C * HD) // T
    dom, x = lax.axis_index("dom"), lax.axis_index("feat")
    c = lax.rem(dom, C)
    z = lax.rem(lax.div(dom, C), Z)
    y = lax.div(dom, C * Z)
    yc = y * C + c

    def at(yy, zz, cc):
        return ((yy * Z + zz) * C + cc, x)

    gyc = Group(Y * C, yc, lambda p: at(lax.div(p, C), z, lax.rem(p, C)))
    gz = Group(Z, z, lambda p: at(y, p, c))
    gy = Group(Y, y, lambda p: at(p, z, c))
    gc = Group(C, c, lambda p: at(y, z, p))
    gx = Group(X, x, lambda p: (dom, p))

    fetch = pltpu.make_async_copy(tiles, tile_buf, tile_sem)
    fetch.start()

    barrier = pltpu.get_barrier_semaphore()
    for group in (gyc, gz, gx):
        group.each(
            lambda step, peer, group=group: pl.semaphore_signal(
                barrier, inc=1, device_id=group.device(peer), device_id_type=pl.DeviceIdType.MESH
            )
        )

    def pick(i, carry):
        rows = pl.ds(pl.multiple_of(i * T, T), T)
        hot = (idx_col[rows, :] == lax.broadcasted_iota(jnp.int32, (T, N), 1)).astype(BF16)
        out_halo[rows, :] = dot(hot, nf[...]).astype(BF16)
        return carry

    lax.fori_loop(0, HALO // T, pick, 0)
    hub_hot = (
        idx_col[pl.ds(HALO, HD), :] == lax.broadcasted_iota(jnp.int32, (HD, N), 1)
    ).astype(BF16)
    hub[y, z, c] = dot(hub_hot, nf[...]).astype(BF16)
    pl.semaphore_wait(barrier, Y * C + Z + X - 3)

    def rows_of(p):
        return pl.ds(pl.multiple_of(p * R, R), R)

    def cols_of(p):
        return pl.ds(pl.multiple_of(p * F, F), F)

    ZC = Z * CUT
    YCC = Y * C * CUT
    ex_yc = Exchange(
        gyc,
        lambda p: out_halo.at[pl.ds(pl.multiple_of(p * ZC, ZC), ZC)],
        lambda p: st1.at[p],
        s_yc,
    )
    ex_hz = Exchange(gz, lambda p: hub.at[y, z, c], lambda p: hub.at[y, p, c], s_hz)
    ex_yc.start()
    ex_hz.start()
    st1[yc] = out_halo[pl.ds(pl.multiple_of(yc * ZC, ZC), ZC), :]

    half = D
    wrows = pl.ds(pl.multiple_of(c * half, half), half)
    ex_xs = Exchange(
        gx, lambda p: nf.at[rows_of(p)], lambda p: selfc.at[:, cols_of(p)], s_xs
    )
    ex_xw = Exchange(
        gx, lambda p: weight.at[wrows], lambda p: wfull.at[wrows, cols_of(p)], s_xw
    )
    ex_xo = Exchange(
        gx, lambda p: out_grad.at[rows_of(p)], lambda p: ogc.at[:, cols_of(p)], s_xo
    )
    ex_xb = Exchange(gx, lambda p: bias, lambda p: biasc.at[:, cols_of(p)], s_xb)
    ex_xs.start()
    ex_xw.start()
    ex_xb.start()
    ex_xo.start()
    selfc[:, cols_of(x)] = nf[rows_of(x), :]
    ogc[:, cols_of(x)] = out_grad[rows_of(x), :]
    wfull[:, cols_of(x)] = weight[...]
    biasc[:, cols_of(x)] = bias[...]

    fetch.wait()
    acc_tiles[NT] = jnp.zeros((T, T), BF16)
    acc_tiles_t[NT] = jnp.zeros((T, T), BF16)

    def add_tile(t, carry):
        value = tile_buf[t].astype(F32) + acc_tiles[prev[t]].astype(F32)
        acc_tiles[t] = value.astype(BF16)
        acc_tiles_t[t] = value.T.astype(BF16)
        return carry

    lax.fori_loop(0, NT, add_tile, 0)

    def perm(rows, source_of):
        r = lax.broadcasted_iota(jnp.int32, (rows, rows), 0)
        i = lax.broadcasted_iota(jnp.int32, (rows, rows), 1)
        return (source_of(r) == i).astype(BF16)

    def log2(n):
        return n.bit_length() - 1

    def div_(a, n):
        return lax.shift_right_logical(a, log2(n))

    def mod_(a, n):
        return a & (n - 1)

    def z_major(r):
        return (mod_(div_(r, CUT), Y * C) * Z + div_(r, YCC)) * CUT + mod_(r, CUT)

    def yc_major(r):
        return (mod_(div_(r, CUT), Z) * (Y * C) + div_(r, ZC)) * CUT + mod_(r, CUT)

    def to_dom(r):
        yy = div_(r, Z * C * CUT)
        zz = mod_(div_(r, C * CUT), Z)
        return (zz * Y + yy) * (C * CUT) + mod_(r, C * CUT)

    def from_dom(r):
        zz = div_(r, Y * C * CUT)
        yy = mod_(div_(r, C * CUT), Y)
        return (yy * Z + zz) * (C * CUT) + mod_(r, C * CUT)

    ex_yc.wait()
    halo_z[...] = (
        dot(perm(HALO, z_major), st1[...].reshape(HALO, F)).astype(BF16).reshape(Z, YCC, F)
    )
    ex_z = Exchange(gz, lambda p: halo_z.at[p], lambda p: st2.at[p], s_z)
    ex_z.start()
    st2[z] = halo_z[z]

    ex_hz.wait()
    ex_hy = Exchange(gy, lambda p: hub.at[y, :, c], lambda p: hub.at[p, :, c], s_hy)
    ex_hy.start()

    def hub_to_core(yy):
        return pltpu.make_async_remote_copy(
            src_ref=hub.at[yy, :, c],
            dst_ref=hub.at[yy, :, c],
            send_sem=s_hc.at[0, yy],
            recv_sem=s_hc.at[1, yy],
            device_id=gc.device(1 - c),
            device_id_type=pl.DeviceIdType.MESH,
        )

    def hub_from_core(yy):
        return pltpu.make_async_remote_copy(
            src_ref=hub.at[yy, :, 1 - c],
            dst_ref=hub.at[yy, :, 1 - c],
            send_sem=s_hc.at[0, yy],
            recv_sem=s_hc.at[1, yy],
            device_id=gc.device(1 - c),
            device_id_type=pl.DeviceIdType.MESH,
        )

    hub_to_core(y).start()

    def place(k, carry):
        for h in range(2):
            for n in range(NB):
                slot = last[n * SB + 2 * k + h]
                adj[k, n * T : (n + 1) * T, h * T : (h + 1) * T] = acc_tiles[slot]
                adj_t[k, h * T : (h + 1) * T, n * T : (n + 1) * T] = acc_tiles_t[slot]
        return carry

    lax.fori_loop(0, SB // 2, place, 0)

    gy.each(lambda step, peer: (ex_hy.wait_one(step, peer), hub_to_core(peer).start())[0])

    ones = jnp.ones((2 * T, F), BF16)
    deg[...] = jnp.zeros_like(deg)
    acc[...] = jnp.zeros_like(acc)

    def add_deg(k, carry):
        deg[...] += dot(adj[k], ones)
        return carry

    lax.fori_loop(0, SB // 2, add_deg, 0)
    deg[...] = 1.0 / jnp.maximum(deg[...], 1.0)
    inv_rows = deg[rows_of(x), :]

    def add_own(k, carry):
        acc[...] += dot(adj[k], nf[pl.ds(pl.multiple_of(k * 2 * T, 2 * T), 2 * T), :])
        return carry

    own_k = NB // 2
    lax.fori_loop(0, own_k, add_own, 0)

    ex_z.wait()
    halo[...] = dot(perm(HALO, to_dom), st2[...].reshape(HALO, F)).astype(BF16)
    halo_k = HALO // (2 * T)

    def add_halo(k, carry):
        acc[...] += dot(adj[own_k + k], halo[pl.ds(pl.multiple_of(k * 2 * T, 2 * T), 2 * T), :])
        return carry

    lax.fori_loop(0, halo_k, add_halo, 0)
    hub_first = own_k + halo_k
    zstep = 2 * T // (C * HD)
    per_y = Z // zstep

    def add_hub(k, carry):
        rows = hub[lax.div(k, per_y), pl.ds(lax.rem(k, per_y) * zstep, zstep)]
        acc[...] += dot(adj[hub_first + k], rows.reshape(2 * T, F))
        return carry

    hub_from_core(y).wait_recv()
    gy.each(lambda step, peer: hub_from_core(peer).wait_recv())
    lax.fori_loop(0, Y * per_y, add_hub, 0)
    mean[...] = (acc[...] * deg[...]).astype(BF16)

    ex_xm = Exchange(
        gx, lambda p: mean.at[rows_of(p)], lambda p: meanc.at[:, cols_of(p)], s_xm
    )
    ex_xm.start()
    meanc[:, cols_of(x)] = mean[rows_of(x), :]

    def w_core(p, cc, step):
        part = wfull.at[pl.ds(pl.multiple_of(cc * half, half), half), cols_of(p)]
        return pltpu.make_async_remote_copy(
            src_ref=part,
            dst_ref=part,
            send_sem=s_wc.at[0, p],
            recv_sem=s_wc.at[1, p],
            device_id=gc.device(1 - c),
            device_id_type=pl.DeviceIdType.MESH,
        )

    gx.each(
        lambda step, peer: (ex_xw.wait_one(step, peer), w_core(peer, c, step).start())[0]
    )
    ex_xs.wait()
    ex_xb.wait()
    ex_xo.wait()
    gx.each(lambda step, peer: w_core(peer, 1 - c, step).wait_recv())
    pre[...] = dot(selfc[...], wfull[0:D, :]) + biasc[0:1, :]
    ex_xm.wait()
    pre_act = pre[...] + dot(meanc[...], wfull[D : 2 * D, :])
    sig = jax.nn.sigmoid(pre_act)
    lo_send[...] = (pre_act * sig).astype(BF16)
    gp[...] = (ogc[...].astype(F32) * (sig * (1.0 + pre_act * (1.0 - sig)))).astype(BF16)
    cat_mean = dot_nt(gp[...], wfull[D : 2 * D, :])
    for j in range(X):
        gm_send[j] = (cat_mean[:, j * F : (j + 1) * F] * inv_rows).astype(BF16)
    ex_xg = Exchange(gx, lambda p: gm_send.at[p], lambda p: gm.at[p], s_xg)
    ex_xg.start()
    gm[x] = gm_send[x]

    for q in range(2 * D // T):
        src = selfc if q * T < D else meanc
        col = (q * T) % D
        part = dot_tn(src[:, col : col + T], gp[...])
        row = (q * T) % D
        wg32[q * T // D, row : row + T, :] = part
        wgb[q * T // D, row : row + T, :] = part.astype(BF16)
    ex_gc = Exchange(gc, lambda p: wgb.at[p], lambda p: wg_core.at[p], s_gc)
    ex_gc.start()
    ex_xl = Exchange(
        gx, lambda p: lo_send.at[:, cols_of(p)], lambda p: lo_recv.at[p], s_xl
    )
    ex_xl.start()
    lo_recv[x] = lo_send[:, cols_of(x)]
    bias_sum = jnp.sum(gp[...].astype(F32), axis=0, keepdims=True)

    def bias_rows(value):
        full = jnp.broadcast_to(value, (8, F))
        high = full.astype(BF16)
        low = (full - high.astype(F32)).astype(BF16)
        return jnp.concatenate([high.astype(F32), low.astype(F32)], axis=0).astype(BF16)

    def bias_of(rows):
        wide = rows.astype(F32)
        return wide[0:8] + wide[8:16]

    cat_self = dot_nt(gp[...], wfull[0:D, :])
    for j in range(X):
        gs_send[j] = cat_self[:, j * F : (j + 1) * F].astype(BF16)
    ex_xgs = Exchange(gx, lambda p: gs_send.at[p], lambda p: gs_recv.at[p], s_xgs)
    ex_xgs.start()
    gs_recv[x] = gs_send[x]

    ex_xg.wait()
    def spread(k):
        return dot(adj_t[k], gm[...].reshape(N, F))

    class Core:
        def __init__(self, yy):
            self.yy = yy

        def copy(self):
            return pltpu.make_async_remote_copy(
                src_ref=hsb.at[1 - c, self.yy],
                dst_ref=hs_core.at[self.yy],
                send_sem=s_bhc.at[0, self.yy],
                recv_sem=s_bhc.at[1, self.yy],
                device_id=gc.device(1 - c),
                device_id_type=pl.DeviceIdType.MESH,
            )

    for yy in range(Y):

        def back_hub(k, carry, yy=yy):
            rows = spread(hub_first + yy * per_y + k).reshape(zstep, C, HD, F)
            for cc in range(C):
                hs32[cc, yy, pl.ds(k * zstep, zstep)] = rows[:, cc]
                hsb[cc, yy, pl.ds(k * zstep, zstep)] = rows[:, cc].astype(BF16)
            return carry

        lax.fori_loop(0, per_y, back_hub, 0)
        Core(yy).copy().start()

    def back_halo(k, carry):
        halo_b[pl.ds(pl.multiple_of(k * 2 * T, 2 * T), 2 * T), :] = spread(own_k + k).astype(BF16)
        return carry

    lax.fori_loop(0, halo_k, back_halo, 0)
    halo_zb[...] = dot(perm(HALO, from_dom), halo_b[...]).astype(BF16).reshape(Z, YCC, F)
    ex_rz = Exchange(gz, lambda p: halo_zb.at[p], lambda p: rt1.at[p], s_rz)
    ex_rz.start()
    rt1[z] = halo_zb[z]

    ex_bhy = Exchange(gy, lambda p: hy_send.at[p], lambda p: hy_recv.at[p], s_bhy)
    for yy in range(Y):
        Core(yy).copy().wait_recv()
        pair = hs32[c, yy] + hs_core[yy].astype(F32)
        hy_own[yy] = pair
        hy_send[yy] = pair.astype(BF16)
    ex_bhy.start()

    ex_gc.wait()
    for j in range(X):
        block = wg32[c, :, j * F : (j + 1) * F] + wg_core[1 - c, :, j * F : (j + 1) * F].astype(F32)
        wx_own[j, 0:D, :] = block
        wx_send[j, 0:D, :] = block.astype(BF16)
        bias_j = bias_sum[:, j * F : (j + 1) * F]
        wx_own[j, D : D + 8, :] = jnp.broadcast_to(bias_j, (8, F))
        wx_send[j, D : D + 16, :] = bias_rows(bias_j)
    ex_gx = Exchange(gx, lambda p: wx_send.at[p], lambda p: wx_recv.at[p], s_gx)
    ex_gx.start()

    def back_own(k, carry):
        rows = pl.ds(pl.multiple_of(k * 2 * T, 2 * T), 2 * T)
        total[rows, :] = spread(k)
        return carry

    lax.fori_loop(0, own_k, back_own, 0)

    ex_rz.wait()
    halo_m[...] = (
        dot(perm(HALO, yc_major), rt1[...].reshape(HALO, F)).astype(BF16).reshape(Y * C, ZC, F)
    )
    ex_ryc = Exchange(gyc, lambda p: halo_m.at[p], lambda p: rt2.at[p], s_ryc)
    ex_ryc.start()
    rt2[yc] = halo_m[yc]

    ex_bhy.wait()
    hy_recv[y] = jnp.zeros((Z, HD, F), BF16)
    hub_y = hy_own[y]
    for yy in range(Y):
        hub_y = hub_y + hy_recv[yy].astype(F32)
    hy_own[y] = hub_y
    hz_send[...] = hub_y.astype(BF16)
    ex_bhz = Exchange(gz, lambda p: hz_send.at[p], lambda p: hz_recv.at[p], s_bhz)
    ex_bhz.start()

    ex_gx.wait()
    wx_recv[x] = jnp.zeros((D + 16, F), BF16)
    wsum = wx_own[x, 0:D, :]
    bsum = wx_own[x, D : D + 8, :]
    for j in range(X):
        wsum = wsum + wx_recv[j, 0:D, :].astype(F32)
        bsum = bsum + bias_of(wx_recv[j, D : D + 16, :])
    DY = D // Y
    for j in range(Y):
        block = wsum[j * DY : (j + 1) * DY]
        wy_own[j] = block
        wy_send[j, 0:DY, :] = block.astype(BF16)
        wy_send[j, DY : DY + 16, :] = bias_rows(bsum[0:1])
    ex_gy = Exchange(gy, lambda p: wy_send.at[p], lambda p: wy_recv.at[p], s_gy)
    ex_gy.start()

    ex_xl.wait()
    for j in range(X):
        layer_out[j * R : (j + 1) * R, :] = lo_recv[j]
    ex_xgs.wait()
    for j in range(X):
        total[j * R : (j + 1) * R, :] += gs_recv[j].astype(F32)

    ex_gy.wait()
    wy_recv[y] = jnp.zeros((DY + 16, F), BF16)
    wsum = wy_own[y]
    for j in range(Y):
        wsum = wsum + wy_recv[j, 0:DY, :].astype(F32)
        bsum = bsum + bias_of(wy_recv[j, DY : DY + 16, :])
    DZ = DY // Z
    for j in range(Z):
        wz_send[j, 0:DZ, :] = wsum[j * DZ : (j + 1) * DZ]
        wz_send[j, DZ : DZ + 8, :] = bsum
    ex_gz = Exchange(gz, lambda p: wz_send.at[p], lambda p: wz_recv.at[p], s_gz)
    ex_gz.start()

    ex_ryc.wait()
    ex_bhz.wait()
    hz_recv[z] = jnp.zeros((HD, F), BF16)
    hub_mine = hy_own[y, z] + jnp.sum(hz_recv[...].astype(F32), axis=0)
    high = hub_mine.astype(BF16)
    low = (hub_mine - high.astype(F32)).astype(BF16)

    ex_gz.wait()
    wz_recv[z] = wz_send[z]
    zsum = jnp.sum(wz_recv[...], axis=0) * scale
    wout[c, y, z] = zsum[0:DZ]
    bias_core[c] = zsum[DZ : DZ + 8]
    ex_az = Exchange(gz, lambda p: wout.at[c, y, z], lambda p: wout.at[c, y, p], s_az)
    ex_az.start()
    ex_bc = Exchange(gc, lambda p: bias_core.at[c], lambda p: bias_core.at[p], s_bc)
    ex_bc.start()

    hot_all = idx_row[...]
    returned = jnp.concatenate([rt2[...].reshape(HALO, F), high, low], axis=0)
    for n in range(NB):
        hot = (
            lax.broadcasted_iota(jnp.int32, (T, HALO + 2 * HD), 0) + n * T == hot_all
        ).astype(BF16)
        rows = total[n * T : (n + 1) * T, :] + dot(hot, returned)
        node_grad[n * T : (n + 1) * T, :] = rows.astype(BF16)

    ex_az.wait()
    ex_ay = Exchange(gy, lambda p: wout.at[c, y], lambda p: wout.at[c, p], s_ay)
    ex_ay.start()
    ex_ay.wait()
    ex_ac = Exchange(gc, lambda p: wout.at[c], lambda p: wout.at[p], s_ac)
    ex_ac.start()
    ex_bc.wait()
    bias_grad[...] = bias_core[0] + bias_core[1]
    ex_ac.wait()
    weight_grad[...] = wout[...].reshape(2 * D, F)

    for ex in (
        ex_yc, ex_z, ex_hz, ex_hy, ex_xs, ex_xw, ex_xo, ex_xb, ex_xm, ex_xl, ex_xg, ex_xgs,
        ex_gc, ex_gx, ex_gy, ex_gz, ex_az, ex_ay, ex_ac, ex_bc, ex_bhy, ex_bhz, ex_rz, ex_ryc,
    ):
        ex.drain()
    for yy in range(Y):
        Core(yy).copy().wait_send()
        hub_to_core(yy).wait_send()
    gx.each(lambda step, peer: w_core(peer, c, step).wait_send())


def per_device(
    sizes,
    node_feats,
    neigh_weight,
    bias,
    out_grad,
    tile_values,
    tile_src,
    tile_dst,
    tile_count,
    hub_rows,
    send_rows,
):
    Y, Z, C, X = sizes
    N, F = node_feats.shape
    NT, T = tile_values.shape[:2]
    CUT = send_rows.shape[1]
    HD = hub_rows.shape[0]
    DOM = Y * Z * C
    HALO = DOM * CUT
    NB, SB = N // T, (N + HALO + DOM * HD) // T
    D, R = X * F, N // X
    K = SB // 2
    ZC, YCC = Z * CUT, Y * C * CUT
    DY = D // Y
    DZ = DY // Z

    at = jnp.arange(NT, dtype=jnp.int32)
    key = jnp.where(at < tile_count[0], tile_dst * SB + tile_src, -1)
    same = (key[:, None] == key[None, :]) & (at[None, :] < at[:, None])
    prev = jnp.max(jnp.where(same, at[None, :], -1), axis=1)
    prev = jnp.where(prev < 0, NT, prev)
    place = jnp.arange(NB * SB, dtype=jnp.int32)
    last = jnp.max(jnp.where(place[:, None] == key[None, :], at[None, :], -1), axis=1)
    last = jnp.where(last < 0, NT, last)
    sends = send_rows.reshape(Y, Z, C, CUT).transpose(0, 2, 1, 3).reshape(HALO)
    idx_col = jnp.concatenate([sends, hub_rows])[:, None]
    idx_row = jnp.concatenate([sends, hub_rows, hub_rows])[None, :]
    bias8 = jnp.broadcast_to(bias[None, :], (8, F))

    dims = (Y, Z, C, X, N, T, NT, F, HD, CUT, 1.0 / math.sqrt(N * DOM))
    vm = pl.BlockSpec(memory_space=pltpu.VMEM)
    sm = pl.BlockSpec(memory_space=pltpu.SMEM)
    anyspace = pl.BlockSpec(memory_space=pl.ANY)

    def b(*shape):
        return pltpu.VMEM(shape, BF16)

    def f(*shape):
        return pltpu.VMEM(shape, F32)

    def sem(n):
        return pltpu.SemaphoreType.DMA((2, n))

    scratch = dict(
        tile_buf=b(NT, T, T),
        acc_tiles=b(NT + 1, T, T),
        acc_tiles_t=b(NT + 1, T, T),
        adj=b(K, N, 2 * T),
        adj_t=b(K, 2 * T, N),
        out_halo=b(HALO, F),
        st1=b(Y * C, ZC, F),
        st2=b(Z, YCC, F),
        halo_z=b(Z, YCC, F),
        halo=b(HALO, F),
        hub=b(Y, Z, C, HD, F),
        deg=f(N, F),
        acc=f(N, F),
        selfc=b(R, D),
        meanc=b(R, D),
        ogc=b(R, D),
        wfull=b(2 * D, D),
        biasc=f(8, D),
        mean=b(N, F),
        pre=f(R, D),
        lo_send=b(R, D),
        lo_recv=b(X, R, F),
        gp=b(R, D),
        gm_send=b(X, R, F),
        gm=b(X, R, F),
        gs_send=b(X, R, F),
        gs_recv=b(X, R, F),
        wg32=f(C, D, D),
        wgb=b(C, D, D),
        wg_core=b(C, D, D),
        wx_send=b(X, D + 16, F),
        wx_recv=b(X, D + 16, F),
        wx_own=f(X, D + 8, F),
        wy_send=b(Y, DY + 16, F),
        wy_recv=b(Y, DY + 16, F),
        wy_own=f(Y, DY, F),
        wz_send=f(Z, DZ + 8, F),
        wz_recv=f(Z, DZ + 8, F),
        wout=f(C, Y, Z, DZ, F),
        bias_core=f(C, 8, F),
        hs32=f(C, Y, Z, HD, F),
        hsb=b(C, Y, Z, HD, F),
        hs_core=b(Y, Z, HD, F),
        hy_send=b(Y, Z, HD, F),
        hy_recv=b(Y, Z, HD, F),
        hy_own=f(Y, Z, HD, F),
        hz_send=b(Z, HD, F),
        hz_recv=b(Z, HD, F),
        halo_b=b(HALO, F),
        halo_zb=b(Z, YCC, F),
        rt1=b(Z, YCC, F),
        halo_m=b(Y * C, ZC, F),
        rt2=b(Y * C, ZC, F),
        total=f(N, F),
        tile_sem=pltpu.SemaphoreType.DMA,
        s_yc=sem(Y * C),
        s_z=sem(Z),
        s_hz=sem(Z),
        s_hy=sem(Y),
        s_hc=sem(Y),
        s_xs=sem(X),
        s_xo=sem(X),
        s_xw=sem(X),
        s_xb=sem(X),
        s_wc=sem(X),
        s_xm=sem(X),
        s_xl=sem(X),
        s_xg=sem(X),
        s_xgs=sem(X),
        s_gc=sem(C),
        s_gx=sem(X),
        s_gy=sem(Y),
        s_gz=sem(Z),
        s_az=sem(Z),
        s_ay=sem(Y),
        s_ac=sem(C),
        s_bc=sem(C),
        s_bhc=sem(Y),
        s_bhy=sem(Y),
        s_bhz=sem(Z),
        s_rz=sem(Z),
        s_ryc=sem(Y * C),
    )
    layer_out, node_grad, weight_grad, bias_grad = pl.pallas_call(
        functools.partial(kernel, dims),
        out_shape=(
            jax.ShapeDtypeStruct((N, F), BF16),
            jax.ShapeDtypeStruct((N, F), BF16),
            jax.ShapeDtypeStruct((2 * D, F), F32),
            jax.ShapeDtypeStruct((8, F), F32),
        ),
        in_specs=[vm, vm, vm, vm, anyspace, vm, vm, sm, sm],
        out_specs=(vm, vm, vm, vm),
        scratch_shapes=list(scratch.values()),
        compiler_params=pltpu.CompilerParams(
            collective_id=0, has_side_effects=True, vmem_limit_bytes=60 * 1024 * 1024
        ),
    )(node_feats, neigh_weight, bias8, out_grad, tile_values, idx_col, idx_row, prev, last)
    return layer_out, node_grad, weight_grad, bias_grad[0]


def solution(mesh, y_chips=Y_CHIPS):
    dom, feat = mesh.shape["dom"], mesh.shape["feat"]
    sizes = (y_chips, dom // (CORES * y_chips), CORES, feat)
    in_specs = (
        P("dom", "feat"),
        P(None, "feat"),
        P("feat"),
        P("dom", "feat"),
        P("dom", None, None),
        P("dom"),
        P("dom"),
        P("dom"),
        P("dom"),
        P("dom", None),
    )
    out_specs = (P("dom", "feat"), P("dom", "feat"), P(None, "feat"), P("feat"))
    return jax.shard_map(
        functools.partial(per_device, sizes),
        mesh=mesh,
        in_specs=in_specs,
        out_specs=out_specs,
        check_vma=False,
    )
```

time: 863 us -> 129 us (0.15); the launches traced: 852 us -> 128 us
  waiting for transfers between devices: 467 us -> 0 us
  blocking collectives: 249 us -> 0 us
  Pallas kernels: 0 us -> 113 us
  starting transfers between devices: 37.3 us -> 0 us
  matrix products: 32.3 us -> 0 us
  local copies, waits for them, and re-layouts: 33.1 us -> 9.96 us
  other arithmetic: 18 us -> 3.54 us
  between operations: 15 us -> 1.3 us
    psum x1 -> x0, blocking collectives: 249 us -> none  [per_device(): weight_sum, bias_sum = lax.psum((local_weight, local_bias), 'dom')]
    reduce_scatter x1 -> x0, waiting for transfers between devices: 244 us -> none  [per_device(): lax.psum_scatter(hub_grad, 'dom', scatter_dimension=0, tiled=True)]
    all_gather x4 -> x0, waiting for transfers between devices: 148 us -> none  [the longest x1 96 us: per_device(): hub_table = lax.all_gather(node_feats[hub_rows], 'dom', axis=0, tiled=True)]
    pallas_call x0 -> x1, Pallas kernels: none -> 113 us  [per_device(): pl.pallas_call(functools.partial(kernel, dims), out_shape=(jax.ShapeDtype...]
    psum x1 -> x0, waiting for transfers between devices: 51.5 us -> none  [per_device(): weight_sum, bias_sum = lax.psum((local_weight, local_bias), 'dom')]
    all_to_all x4 -> x0, starting transfers between devices: 36.9 us -> none  [the longest x1 20.6 us: per_device(): lax.all_to_all(outgoing, 'dom', split_axis=0, concat_axis=0, tiled=True)]
    dot_general x10 -> x0, matrix products: 32.3 us -> none  [the longest x1 6.47 us: per_device(): jnp.einsum('tij,tjf->tif', tile_values, picked, preferred_element_type=jn...]
    all_to_all x4 -> x0, waiting for transfers between devices: 22.6 us -> none  [the longest x1 13.2 us: per_device(): lax.all_to_all(outgoing, 'dom', split_axis=0, concat_axis=0, tiled=True)]
  transfers between devices with their start and end apart: 10 -> 0, of which waited for: 9 -> 0; matrix products, arithmetic and copies ran while one was open for 9% -> 0% of each run, Pallas kernels for 0% -> 0%
where the time goes in v1:
time: 129 us; the launch traced here: 128 us
  Pallas kernels  113 us (88%)
  local copies, waits for them, and re-layouts  9.96 us (8%)
  other arithmetic  3.54 us (3%)
  between operations  1.3 us (1%)
    pallas_call x1, Pallas kernels, per_device(): pl.pallas_call(functools.partial(kernel, dims), out_shape=(jax.ShapeDtype...  113 us
    unnamed x4, local copies, waits for them, and re-layouts  5.99 us

profile of v1, /device:TPU:1, one launch (start us, length us, event | category | flops | bytes accessed | tf_op | source)
XLA Modules:
  0.0 128.3 jit_solution(7708677122328199653)
XLA Ops:
  1.3 0.7 compare_select_fusion.2
  2.0 0.2 select_reduce_fusion.1
  2.1 0.5 compare_select_fusion.1.prev
  2.7 0.1 select_reduce_fusion
  2.8 0.6 compare_select_fusion.last
  3.4 1.2 broadcast_in_dim.54.bias
  4.6 0.8 copy.17
  5.4 0.1 reshape.18
  5.5 0.8 pad_add_fusion.1
  6.3 0.6 broadcast_in_dim.56.idx_row
  6.9 0.7 pad_add_fusion
  7.6 0.8 broadcast_in_dim.63.idx_col
  8.4 113.5 %shard_map.129 = (bf16[1024,128]{1,0:T(8,128)(2,1)}, bf16[1024,128]{1,0:T(8,128)(2,1)}, f32[1024,128]{1,0:T(8,128)}, f32[8,128]{1,0:T(8,128)}) custom-call(bf16[1024,128]{1,0:T(8,128)(2,1)} %nf.1, bf16[1024,128]{1,0:T(8,128)(2,1)} %weight.1, f32[8,128]{1,0:T(8,128)} %broadcast_in_dim.54.bias, bf16[1024,128]{1,0:T(8,128)(2,1)} %out_grad.1, ...), custom_call_target="tpu_custom_call" | custom-call | tf_op jit(solution)/shard_map/pallas_call | solution.py:765
  121.9 1.2 slice_bitcast_fusion
  123.1 1.7 %copy.24 = bf16[1024,128]{1,0:T(8,128)(2,1)} copy(bf16[1024,128]{1,0:T(8,128)(2,1)} %get-tuple-element.16) | data formatting | bytes 524288
  124.7 1.7 %copy.25 = bf16[1024,128]{1,0:T(8,128)(2,1)} copy(bf16[1024,128]{1,0:T(8,128)(2,1)} %get-tuple-element.17) | data formatting | bytes 524288
  126.4 1.9 %copy.26 = f32[1024,128]{1,0:T(8,128)} copy(f32[1024,128]{1,0:T(8,128)} %get-tuple-element.18) | data formatting | bytes 1048576
  (1 shorter events, 0.0 us)

commit v2 on v0

v2 whole, which is shorter than its diff:
```python
import functools
import math
import types

import jax
import jax.numpy as jnp
from jax import lax
from jax.experimental import pallas as pl
from jax.experimental.pallas import tpu as pltpu
from jax.sharding import PartitionSpec as P

BF16 = jnp.bfloat16
F32 = jnp.float32
CORES = 2
Y_CHIPS = 4


def dot(a, b):
    return jnp.dot(a, b, preferred_element_type=F32)


def dot_nt(a, b):
    return lax.dot_general(a, b, (((1,), (1,)), ((), ())), preferred_element_type=F32)


def dot_tn(a, b):
    return lax.dot_general(a, b, (((0,), (0,)), ((), ())), preferred_element_type=F32)


class Group:
    def __init__(self, size, me, device):
        self.size, self.me, self.device = size, me, device

    def each(self, body):
        if self.size <= 4:
            for step in range(1, self.size):
                body(step, lax.rem(self.me + step, self.size))
        else:

            def loop(step, carry):
                body(step, lax.rem(self.me + step, self.size))
                return carry

            lax.fori_loop(1, self.size, loop, 0)


class Exchange:
    def __init__(self, group, src, dst, sems):
        self.group, self.src, self.dst, self.sems = group, src, dst, sems

    def copy(self, step, peer, landing):
        return pltpu.make_async_remote_copy(
            src_ref=self.src(peer),
            dst_ref=self.dst(landing),
            send_sem=self.sems.at[0, step],
            recv_sem=self.sems.at[1, landing],
            device_id=self.group.device(peer),
            device_id_type=pl.DeviceIdType.MESH,
        )

    def start_to(self, peer):
        step = lax.rem(peer - self.group.me + self.group.size, self.group.size)
        self.copy(step, peer, self.group.me).start()

    def start_one(self, step, peer):
        self.copy(step, peer, self.group.me).start()

    def start(self):
        self.group.each(self.start_one)

    def wait_one(self, step, peer):
        self.copy(step, peer, peer).wait_recv()

    def wait(self):
        self.group.each(self.wait_one)

    def wait_then(self, after):
        def body(step, peer):
            self.wait_one(step, peer)
            after(peer)

        self.group.each(body)

    def drain(self):
        self.group.each(lambda step, peer: self.copy(step, peer, self.group.me).wait_send())


class Relay:
    def __init__(self, device, sems, src, dst):
        self.device, self.sems, self.src, self.dst = device, sems, src, dst

    def copy(self, slot):
        return pltpu.make_async_remote_copy(
            src_ref=self.src(slot),
            dst_ref=self.dst(slot),
            send_sem=self.sems.at[0, slot],
            recv_sem=self.sems.at[1, slot],
            device_id=self.device,
            device_id_type=pl.DeviceIdType.MESH,
        )

    def start(self, slot):
        self.copy(slot).start()


def log2(n):
    return n.bit_length() - 1


def div_(a, n):
    return lax.shift_right_logical(a, log2(n))


def mod_(a, n):
    return a & (n - 1)


def aligned(start, size):
    return pl.ds(pl.multiple_of(start, size), size)


def kernel(dims, names, *refs):
    r = types.SimpleNamespace(**dict(zip(names, refs)))
    Y, Z, C, X, N, T, NT, F, HD, CUT, scale = dims
    D = X * F
    R = N // X
    DOM = Y * Z * C
    HALO = DOM * CUT
    NB = N // T
    SB = (N + HALO + DOM * HD) // T
    ZC, YCC = Z * CUT, Y * C * CUT
    PERY = Z * C * HD
    DY = D // Y
    DZ = DY // Z
    dom, x = lax.axis_index("dom"), lax.axis_index("feat")
    c = lax.rem(dom, C)
    z = lax.rem(lax.div(dom, C), Z)
    y = lax.div(dom, C * Z)
    yc = y * C + c

    def at(yy, zz, cc):
        return ((yy * Z + zz) * C + cc, x)

    gyc = Group(Y * C, yc, lambda p: at(lax.div(p, C), z, lax.rem(p, C)))
    gz = Group(Z, z, lambda p: at(y, p, c))
    gy = Group(Y, y, lambda p: at(p, z, c))
    gc = Group(C, c, lambda p: at(y, z, p))
    gx = Group(X, x, lambda p: (dom, p))
    other_core = at(y, z, 1 - c)

    barrier = pltpu.get_barrier_semaphore()
    for group in (gyc, gz, gx):
        group.each(
            lambda step, peer, group=group: pl.semaphore_signal(
                barrier, inc=1, device_id=group.device(peer), device_id_type=pl.DeviceIdType.MESH
            )
        )

    def rows_of(p):
        return aligned(p * R, R)

    def cols_of(p):
        return aligned(p * F, F)

    def local(i, src, dst):
        return pltpu.make_async_copy(src, dst, r.local_sem.at[i])

    fetch_nf = local(0, r.node_feats, r.nf)
    fetch_tiles = local(1, r.tiles, r.tile_buf)
    fetch_w = local(2, r.weight, r.wv)
    fetch_og = local(3, r.out_grad, r.ogv)
    fetch_nf.start()
    fetch_w.start()
    fetch_og.start()
    fetch_tiles.start()

    eye = lax.broadcasted_iota(jnp.int32, (DOM, DOM), 0) == lax.broadcasted_iota(
        jnp.int32, (DOM, DOM), 1
    )
    for k in range(CUT):
        wide = jnp.broadcast_to(r.sends[k : k + 1, :], (DOM, DOM)).astype(F32)
        col = jnp.sum(jnp.where(eye, wide, 0.0), axis=1, keepdims=True).astype(jnp.int32)
        r.hot[k * DOM : (k + 1) * DOM, :] = (
            col == lax.broadcasted_iota(jnp.int32, (DOM, N), 1)
        ).astype(BF16)
    eye = lax.broadcasted_iota(jnp.int32, (HD, HD), 0) == lax.broadcasted_iota(
        jnp.int32, (HD, HD), 1
    )
    wide = jnp.broadcast_to(r.hub_ids[...], (HD, HD)).astype(F32)
    col = jnp.sum(jnp.where(eye, wide, 0.0), axis=1, keepdims=True).astype(jnp.int32)
    hub_hot = (col == lax.broadcasted_iota(jnp.int32, (HD, N), 1)).astype(BF16)

    def perm(source_of):
        row = lax.broadcasted_iota(jnp.int32, (HALO, HALO), 0)
        lane = lax.broadcasted_iota(jnp.int32, (HALO, HALO), 1)
        return (source_of(row) == lane).astype(BF16)

    def peer_major(i):
        k, zz = mod_(i, CUT), mod_(div_(i, CUT), Z)
        cc, yy = mod_(div_(i, ZC), C), div_(i, ZC * C)
        return k * DOM + (yy * Z + zz) * C + cc

    def z_major(i):
        return (mod_(div_(i, CUT), Y * C) * Z + div_(i, YCC)) * CUT + mod_(i, CUT)

    def yc_major(i):
        return (mod_(div_(i, CUT), Z) * (Y * C) + div_(i, ZC)) * CUT + mod_(i, CUT)

    def to_dom(i):
        yy = div_(i, Z * C * CUT)
        zz = mod_(div_(i, C * CUT), Z)
        return (zz * Y + yy) * (C * CUT) + mod_(i, C * CUT)

    def from_dom(i):
        zz = div_(i, Y * C * CUT)
        yy = mod_(div_(i, C * CUT), Y)
        return (yy * Z + zz) * (C * CUT) + mod_(i, C * CUT)

    fetch_nf.wait()
    r.hub[y, z, c] = dot(hub_hot, r.nf[...]).astype(BF16)
    picked = dot(r.hot[...], r.nf[...]).astype(BF16)
    r.out_halo[...] = dot(perm(peer_major), picked).astype(BF16).reshape(Y * C, ZC, F)
    r.bias8[...] = jnp.broadcast_to(r.bias[...], (8, F))
    pl.semaphore_wait(barrier, Y * C + Z + X - 3)

    done = []

    def exchange(group, src, dst, sems):
        ex = Exchange(group, src, dst, sems)
        done.append(ex)
        return ex

    ex_yc = exchange(gyc, lambda p: r.out_halo.at[p], lambda p: r.st1.at[p], r.s_yc)
    ex_yc.start()
    ex_hz = exchange(gz, lambda p: r.hub.at[y, z, c], lambda p: r.hub.at[y, p, c], r.s_hz)
    ex_hz.start()
    r.st1[yc] = r.out_halo[yc]

    wrows = aligned(c * D, D)
    fetch_w.wait()
    fetch_og.wait()
    ex_xw = exchange(
        gx, lambda p: r.wv.at[wrows], lambda p: r.wfull.at[wrows, cols_of(p)], r.s_xw
    )
    ex_xw.start()
    ex_xs = exchange(
        gx, lambda p: r.nf.at[rows_of(p)], lambda p: r.selfc.at[:, cols_of(p)], r.s_xs
    )
    ex_xs.start()
    ex_xb = exchange(gx, lambda p: r.bias8, lambda p: r.biasc.at[:, cols_of(p)], r.s_xb)
    ex_xb.start()
    ex_xo = exchange(
        gx, lambda p: r.ogv.at[rows_of(p)], lambda p: r.ogc.at[:, cols_of(p)], r.s_xo
    )
    ex_xo.start()
    r.biasc[:, cols_of(x)] = r.bias8[...]
    r.selfc[:, cols_of(x)] = r.nf[rows_of(x), :]
    r.ogc[:, cols_of(x)] = r.ogv[rows_of(x), :]
    r.wfull[:, cols_of(x)] = r.wv[...]

    fetch_tiles.wait()
    r.acc_tiles[0] = jnp.zeros((T, T), BF16)
    r.acc_tiles_t[0] = jnp.zeros((T, T), BF16)

    def add_tile(t, carry):
        value = r.tile_buf[t].astype(F32) + r.acc_tiles[r.prev[t]].astype(F32)
        r.acc_tiles[t + 1] = value.astype(BF16)
        r.acc_tiles_t[t + 1] = value.T.astype(BF16)
        return carry

    lax.fori_loop(0, NT, add_tile, 0)

    ex_yc.wait()
    r.halo_z[...] = (
        dot(perm(z_major), r.st1[...].reshape(HALO, F)).astype(BF16).reshape(Z, YCC, F)
    )
    ex_z = exchange(gz, lambda p: r.halo_z.at[p], lambda p: r.st2.at[p], r.s_z)
    ex_z.start()
    r.st2[z] = r.halo_z[z]

    def place(s, carry):
        for n in range(NB):
            slot = r.last[n * SB + s]
            r.adj[n * T : (n + 1) * T, aligned(s * T, T)] = r.acc_tiles[slot]
            r.adj_t[aligned(s * T, T), n * T : (n + 1) * T] = r.acc_tiles_t[slot]
        return carry

    lax.fori_loop(0, SB, place, 0)

    ex_hz.wait()
    ex_hy = exchange(gy, lambda p: r.hub.at[y, :, c], lambda p: r.hub.at[p, :, c], r.s_hy)
    ex_hy.start()
    hub_to = Relay(other_core, r.s_hc, lambda p: r.hub.at[p, :, c], lambda p: r.hub.at[p, :, c])
    hub_from = Relay(
        other_core, r.s_hc, lambda p: r.hub.at[p, :, 1 - c], lambda p: r.hub.at[p, :, 1 - c]
    )
    hub_to.start(y)

    w_to = Relay(
        other_core,
        r.s_wc,
        lambda p: r.wfull.at[wrows, cols_of(p)],
        lambda p: r.wfull.at[wrows, cols_of(p)],
    )
    other_rows = aligned((1 - c) * D, D)
    w_from = Relay(
        other_core,
        r.s_wc,
        lambda p: r.wfull.at[other_rows, cols_of(p)],
        lambda p: r.wfull.at[other_rows, cols_of(p)],
    )
    def add_deg(n, carry):
        rows = aligned(n * T, T)
        lanes = r.adj[rows, 0:T]
        for s in range(1, SB):
            lanes = lanes + r.adj[rows, s * T : (s + 1) * T]
        r.deg[rows, :] = 1.0 / jnp.maximum(dot(lanes, ones), 1.0)
        return carry

    ones = jnp.ones((T, F), BF16)
    lax.fori_loop(0, NB, add_deg, 0)
    r.acc[...] = dot(r.adj[:, 0:N], r.nf[...])

    def add_hub(p):
        cols = pl.ds(pl.multiple_of(N + HALO + p * PERY, T), PERY)
        r.acc[...] += dot(r.adj[:, cols], r.hub[p].reshape(PERY, F))

    hub_from.copy(y).wait_recv()
    add_hub(y)

    ex_xw.wait_then(w_to.start)
    ex_hy.wait_then(hub_to.start)

    ex_z.wait()
    halo = dot(perm(to_dom), r.st2[...].reshape(HALO, F)).astype(BF16)
    r.acc[...] += dot(r.adj[:, N : N + HALO], halo)

    for i in range(1, Y):
        p = lax.rem(y + i, Y)
        hub_from.copy(p).wait_recv()
        add_hub(p)
    r.mean[...] = (r.acc[...] * r.deg[...]).astype(BF16)
    ex_xm = exchange(
        gx, lambda p: r.mean.at[rows_of(p)], lambda p: r.meanc.at[:, cols_of(p)], r.s_xm
    )
    ex_xm.start()
    r.meanc[:, cols_of(x)] = r.mean[rows_of(x), :]

    ex_xs.wait()
    ex_xb.wait()
    ex_xo.wait()
    gx.each(lambda step, peer: w_from.copy(peer).wait_recv())
    r.pre[...] = dot(r.selfc[...], r.wfull[0:D, :]) + r.biasc[0:1, :]

    for k in range(CUT):
        row = jnp.broadcast_to(r.sends[k : k + 1, :], (N, DOM))
        r.hot_t[:, k * DOM : (k + 1) * DOM] = (
            row == lax.broadcasted_iota(jnp.int32, (N, DOM), 0)
        ).astype(BF16)

    ex_xm.wait()
    pre_act = r.pre[...] + dot(r.meanc[...], r.wfull[D : 2 * D, :])
    sig = jax.nn.sigmoid(pre_act)
    r.gp[...] = (r.ogc[...].astype(F32) * (sig * (1.0 + pre_act * (1.0 - sig)))).astype(BF16)
    r.lo_send[...] = (pre_act * sig).astype(BF16)
    inv_rows = r.deg[rows_of(x), :]
    cat_mean = dot_nt(r.gp[...], r.wfull[D : 2 * D, :])
    for j in range(X):
        r.gm_send[j] = (cat_mean[:, j * F : (j + 1) * F] * inv_rows).astype(BF16)
    ex_xg = exchange(gx, lambda p: r.gm_send.at[p], lambda p: r.gm.at[p], r.s_xg)
    ex_xg.start()
    r.gm[x] = r.gm_send[x]

    for half, src in enumerate((r.selfc, r.meanc)):
        for q in range(0, D, 2 * T):
            part = dot_tn(src[:, q : q + 2 * T], r.gp[...])
            r.wg32[half, q : q + 2 * T, :] = part
            r.wgb[half, q : q + 2 * T, :] = part.astype(BF16)
    ex_gc = exchange(gc, lambda p: r.wgb.at[p], lambda p: r.wg_core.at[p], r.s_gc)
    ex_gc.start()
    bias_sum = jnp.sum(r.gp[...].astype(F32), axis=0, keepdims=True)

    def bias_rows(value):
        full = jnp.broadcast_to(value, (8, F))
        high = full.astype(BF16).astype(F32)
        return jnp.concatenate([high, full - high], axis=0).astype(BF16)

    def bias_of(rows):
        wide = rows.astype(F32)
        return wide[0:8] + wide[8:16]

    cat_self = dot_nt(r.gp[...], r.wfull[0:D, :])
    for j in range(X):
        r.gs_send[j] = cat_self[:, j * F : (j + 1) * F].astype(BF16)
    ex_gc.wait()
    for j in range(X):
        cols = slice(j * F, (j + 1) * F)
        block = r.wg32[c, :, cols] + r.wg_core[1 - c, :, cols].astype(F32)
        r.wx_own[j, 0:D, :] = block
        r.wx_send[j, 0:D, :] = block.astype(BF16)
        r.wx_own[j, D : D + 8, :] = jnp.broadcast_to(bias_sum[:, cols], (8, F))
        r.wx_send[j, D : D + 16, :] = bias_rows(bias_sum[:, cols])
    ex_gx = exchange(gx, lambda p: r.wx_send.at[p], lambda p: r.wx_recv.at[p], r.s_gx)
    ex_gx.start()

    ex_xgs = exchange(gx, lambda p: r.gs_send.at[p], lambda p: r.gs_recv.at[p], r.s_xgs)
    ex_xgs.start()
    ex_xl = exchange(
        gx, lambda p: r.lo_send.at[:, cols_of(p)], lambda p: r.lo_recv.at[p], r.s_xl
    )
    ex_xl.start()
    r.lo_recv[x] = r.lo_send[:, cols_of(x)]
    r.gs_recv[x] = r.gs_send[x]

    ex_xg.wait()
    core_to = Relay(
        other_core, r.s_bhc, lambda p: r.hsb.at[1 - c, p], lambda p: r.hs_core.at[p]
    )
    ex_bhy = exchange(gy, lambda p: r.hy_send.at[p], lambda p: r.hy_recv.at[p], r.s_bhy)

    def spread(rows):
        return dot(r.adj_t[rows, :], r.gm[...].reshape(N, F))

    def back_hub(p):
        rows = spread(pl.ds(pl.multiple_of(N + HALO + p * PERY, T), PERY)).reshape(Z, C, HD, F)
        for cc in range(C):
            r.hs32[cc, p] = rows[:, cc]
            r.hsb[cc, p] = rows[:, cc].astype(BF16)
        core_to.start(p)

    def pair_hub(p, own):
        core_to.copy(p).wait_recv()
        pair = r.hs32[c, p] + r.hs_core[p].astype(F32)
        if own:
            r.hy_own[...] = pair
        else:
            r.hy_send[p] = pair.astype(BF16)
            ex_bhy.start_to(p)

    order = [lax.rem(y + i, Y) for i in range(1, Y)] + [y]
    back_hub(order[0])
    for i in range(1, Y):
        back_hub(order[i])
        pair_hub(order[i - 1], False)

    halo_b = spread(slice(N, N + HALO)).astype(BF16)
    r.halo_zb[...] = dot(perm(from_dom), halo_b).astype(BF16).reshape(Z, YCC, F)
    ex_rz = exchange(gz, lambda p: r.halo_zb.at[p], lambda p: r.rt1.at[p], r.s_rz)
    ex_rz.start()
    r.rt1[z] = r.halo_zb[z]

    pair_hub(y, True)

    r.wx_recv[x] = jnp.zeros((D + 16, F), BF16)
    ex_gx.wait()
    wsum = r.wx_own[x, 0:D, :]
    bsum = r.wx_own[x, D : D + 8, :]
    for j in range(X):
        wsum = wsum + r.wx_recv[j, 0:D, :].astype(F32)
        bsum = bsum + bias_of(r.wx_recv[j, D : D + 16, :])
    for j in range(Y):
        block = wsum[j * DY : (j + 1) * DY]
        r.wy_own[j] = block
        r.wy_send[j, 0:DY, :] = block.astype(BF16)
        r.wy_send[j, DY : DY + 16, :] = bias_rows(bsum[0:1])
    ex_gy = exchange(gy, lambda p: r.wy_send.at[p], lambda p: r.wy_recv.at[p], r.s_gy)
    ex_gy.start()

    r.total[...] = spread(slice(0, N))

    ex_xgs.wait()
    for j in range(X):
        r.total[j * R : (j + 1) * R, :] += r.gs_recv[j].astype(F32)

    r.hy_recv[y] = jnp.zeros((Z, HD, F), BF16)
    ex_bhy.wait()
    hub_y = r.hy_own[...]
    for p in range(Y):
        hub_y = hub_y + r.hy_recv[p].astype(F32)
    r.hy_own[...] = hub_y
    r.hz_send[...] = hub_y.astype(BF16)
    ex_bhz = exchange(gz, lambda p: r.hz_send.at[p], lambda p: r.hz_recv.at[p], r.s_bhz)
    ex_bhz.start()

    ex_rz.wait()
    r.halo_m[...] = (
        dot(perm(yc_major), r.rt1[...].reshape(HALO, F)).astype(BF16).reshape(Y * C, ZC, F)
    )
    ex_ryc = exchange(gyc, lambda p: r.halo_m.at[p], lambda p: r.rt2.at[p], r.s_ryc)
    ex_ryc.start()
    r.rt2[yc] = r.halo_m[yc]

    r.wy_recv[y] = jnp.zeros((DY + 16, F), BF16)
    ex_gy.wait()
    wsum = r.wy_own[y]
    for j in range(Y):
        wsum = wsum + r.wy_recv[j, 0:DY, :].astype(F32)
        bsum = bsum + bias_of(r.wy_recv[j, DY : DY + 16, :])
    for j in range(Z):
        r.wz_send[j, 0:DZ, :] = wsum[j * DZ : (j + 1) * DZ]
        r.wz_send[j, DZ : DZ + 8, :] = bsum
    ex_gz = exchange(gz, lambda p: r.wz_send.at[p], lambda p: r.wz_recv.at[p], r.s_gz)
    ex_gz.start()

    ex_xl.wait()
    lo_out = local(5, r.lo_recv, r.layer_out)
    lo_out.start()

    ex_ryc.wait()
    returned = dot(perm(from_peer_major(dims)), r.rt2[...].reshape(HALO, F)).astype(BF16)
    r.total[...] += dot(r.hot_t[...], returned)

    r.wz_recv[z] = jnp.zeros((DZ + 8, F), F32)
    ex_gz.wait()
    zsum = (jnp.sum(r.wz_recv[...], axis=0) + r.wz_send[z]) * scale
    r.wout[z] = zsum[0:DZ]
    r.bias_core[c] = zsum[DZ : DZ + 8]
    ex_az = exchange(gz, lambda p: r.wout.at[z], lambda p: r.wout.at[p], r.s_az)
    ex_az.start()
    ex_bc = exchange(gc, lambda p: r.bias_core.at[c], lambda p: r.bias_core.at[p], r.s_bc)
    ex_bc.start()

    r.hz_recv[z] = jnp.zeros((HD, F), BF16)
    ex_bhz.wait()
    hub_mine = r.hy_own[z] + jnp.sum(r.hz_recv[...].astype(F32), axis=0)
    high = hub_mine.astype(BF16)
    low = (hub_mine - high.astype(F32)).astype(BF16)
    hub_hot_t = (
        jnp.broadcast_to(r.hub_ids[...], (N, HD)) == lax.broadcasted_iota(jnp.int32, (N, HD), 0)
    ).astype(BF16)
    r.ng[...] = (r.total[...] + dot(hub_hot_t, high) + dot(hub_hot_t, low)).astype(BF16)
    ng_out = local(6, r.ng, r.node_grad)
    ng_out.start()

    ex_az.wait()
    r.wb_all[yc_row(c, Y, y)] = r.wout[...].reshape(DY, F).astype(BF16)
    ex_ay = exchange(
        gyc,
        lambda p: r.wb_all.at[yc_row(c, Y, y)],
        lambda p: r.wb_all.at[yc_row(lax.rem(p, C), Y, lax.div(p, C))],
        r.s_ay,
    )
    ex_ay.start()
    ex_bc.wait()
    r.bias_grad[...] = r.bias_core[0, 0:1] + r.bias_core[1, 0:1]
    ex_ay.wait()
    r.wg_all[...] = r.wb_all[...].astype(F32).reshape(C * Y, Z, DZ, F)
    r.wg_all[yc_row(c, Y, y)] = r.wout[...]

    w_out = local(7, r.wg_all, r.weight_grad)
    w_out.start()
    lo_out.wait()
    ng_out.wait()
    w_out.wait()
    for ex in done:
        ex.drain()
    for p in range(Y):
        hub_to.copy(p).wait_send()
        core_to.copy(p).wait_send()
    gx.each(lambda step, peer: w_to.copy(peer).wait_send())


def yc_row(c, Y, y):
    return c * Y + y


def from_peer_major(dims):
    Y, Z, C, CUT = dims[0], dims[1], dims[2], dims[9]
    DOM = Y * Z * C

    def source(i):
        k, q = div_(i, DOM), mod_(i, DOM)
        cc, zz, yy = mod_(q, C), mod_(div_(q, C), Z), div_(q, C * Z)
        return ((yy * C + cc) * Z + zz) * CUT + k

    return source


def copy_kernel(*refs):
    n = len(refs) // 2
    for src, dst in zip(refs[:n], refs[n:]):
        dst[...] = src[...]


def per_device(
    sizes,
    node_feats,
    neigh_weight,
    bias,
    out_grad,
    tile_values,
    tile_src,
    tile_dst,
    tile_count,
    hub_rows,
    send_rows,
):
    Y, Z, C, X = sizes
    N, F = node_feats.shape
    NT, T = tile_values.shape[:2]
    CUT = send_rows.shape[1]
    HD = hub_rows.shape[0]
    DOM = Y * Z * C
    HALO = DOM * CUT
    NB, SB = N // T, (N + HALO + DOM * HD) // T
    D, R = X * F, N // X
    ZC, YCC = Z * CUT, Y * C * CUT
    DY = D // Y
    DZ = DY // Z

    at = jnp.arange(NT, dtype=jnp.int32)
    key = jnp.where(at < tile_count[0], tile_dst * SB + tile_src, -1)
    same = (key[:, None] == key[None, :]) & (at[None, :] < at[:, None])
    prev = jnp.max(jnp.where(same, at[None, :] + 1, 0), axis=1)
    place = jnp.arange(NB * SB, dtype=jnp.int32)
    last = jnp.max(jnp.where(place[:, None] == key[None, :], at[None, :] + 1, 0), axis=1)

    dims = (Y, Z, C, X, N, T, NT, F, HD, CUT, 1.0 / math.sqrt(N * DOM))
    vm = pl.BlockSpec(memory_space=pltpu.VMEM)
    sm = pl.BlockSpec(memory_space=pltpu.SMEM)
    hbm = pl.BlockSpec(memory_space=pl.ANY)

    def b(*shape):
        return pltpu.VMEM(shape, BF16)

    def f(*shape):
        return pltpu.VMEM(shape, F32)

    def sem(n):
        return pltpu.SemaphoreType.DMA((2, n))

    inputs = dict(
        node_feats=(node_feats, hbm),
        weight=(neigh_weight, hbm),
        out_grad=(out_grad, hbm),
        tiles=(tile_values, hbm),
        bias=(bias[None, :], vm),
        sends=(send_rows.T, vm),
        hub_ids=(hub_rows[None, :], vm),
        prev=(prev, sm),
        last=(last, sm),
    )
    outputs = dict(
        layer_out=(jax.ShapeDtypeStruct((X, R, F), BF16), hbm),
        node_grad=(jax.ShapeDtypeStruct((N, F), BF16), hbm),
        weight_grad=(jax.ShapeDtypeStruct((C * Y, Z, DZ, F), F32), hbm),
        bias_grad=(jax.ShapeDtypeStruct((1, F), F32), vm),
    )
    scratch = dict(
        nf=b(N, F),
        tile_buf=b(NT, T, T),
        acc_tiles=b(NT + 1, T, T),
        acc_tiles_t=b(NT + 1, T, T),
        adj=b(N, SB * T),
        adj_t=b(SB * T, N),
        hot=b(HALO, N),
        hot_t=b(N, HALO),
        out_halo=b(Y * C, ZC, F),
        st1=b(Y * C, ZC, F),
        st2=b(Z, YCC, F),
        halo_z=b(Z, YCC, F),
        hub=b(Y, Z, C, HD, F),
        deg=f(N, F),
        acc=f(N, F),
        selfc=b(R, D),
        meanc=b(R, D),
        ogc=b(R, D),
        wfull=b(2 * D, D),
        bias8=f(8, F),
        biasc=f(8, D),
        mean=b(N, F),
        pre=f(R, D),
        lo_send=b(R, D),
        lo_recv=b(X, R, F),
        wv=b(2 * D, F),
        ogv=b(N, F),
        wg_all=f(C * Y, Z, DZ, F),
        wb_all=b(C * Y, DY, F),
        gp=b(R, D),
        gm_send=b(X, R, F),
        gm=b(X, R, F),
        gs_send=b(X, R, F),
        gs_recv=b(X, R, F),
        wg32=f(C, D, D),
        wgb=b(C, D, D),
        wg_core=b(C, D, D),
        wx_send=b(X, D + 16, F),
        wx_recv=b(X, D + 16, F),
        wx_own=f(X, D + 8, F),
        wy_send=b(Y, DY + 16, F),
        wy_recv=b(Y, DY + 16, F),
        wy_own=f(Y, DY, F),
        wz_send=f(Z, DZ + 8, F),
        wz_recv=f(Z, DZ + 8, F),
        wout=f(Z, DZ, F),
        bias_core=f(C, 8, F),
        hs32=f(C, Y, Z, HD, F),
        hsb=b(C, Y, Z, HD, F),
        hs_core=b(Y, Z, HD, F),
        hy_send=b(Y, Z, HD, F),
        hy_recv=b(Y, Z, HD, F),
        hy_own=f(Z, HD, F),
        hz_send=b(Z, HD, F),
        hz_recv=b(Z, HD, F),
        halo_zb=b(Z, YCC, F),
        rt1=b(Z, YCC, F),
        halo_m=b(Y * C, ZC, F),
        rt2=b(Y * C, ZC, F),
        total=f(N, F),
        ng=b(N, F),
        local_sem=pltpu.SemaphoreType.DMA((8,)),
        s_yc=sem(Y * C),
        s_z=sem(Z),
        s_hz=sem(Z),
        s_hy=sem(Y),
        s_hc=sem(Y),
        s_xs=sem(X),
        s_xo=sem(X),
        s_xw=sem(X),
        s_xb=sem(X),
        s_wc=sem(X),
        s_xm=sem(X),
        s_xl=sem(X),
        s_xg=sem(X),
        s_xgs=sem(X),
        s_gc=sem(C),
        s_gx=sem(X),
        s_gy=sem(Y),
        s_gz=sem(Z),
        s_az=sem(Z),
        s_ay=sem(Y * C),
        s_bc=sem(C),
        s_bhc=sem(Y),
        s_bhy=sem(Y),
        s_bhz=sem(Z),
        s_rz=sem(Z),
        s_ryc=sem(Y * C),
    )
    names = list(inputs) + list(outputs) + list(scratch)
    results = pl.pallas_call(
        functools.partial(kernel, dims, names),
        out_shape=[shape for shape, _ in outputs.values()],
        in_specs=[spec for _, spec in inputs.values()],
        out_specs=[spec for _, spec in outputs.values()],
        scratch_shapes=list(scratch.values()),
        compiler_params=pltpu.CompilerParams(
            collective_id=0, has_side_effects=True, vmem_limit_bytes=60 * 1024 * 1024
        ),
    )(*[array for array, _ in inputs.values()])
    layer_out, node_grad, weight_grad, bias_grad = pl.pallas_call(
        copy_kernel,
        out_shape=[jax.ShapeDtypeStruct(v.shape, v.dtype) for v in results],
        in_specs=[vm] * 4,
        out_specs=[vm] * 4,
    )(*results)
    return (
        layer_out.reshape(N, F),
        node_grad,
        weight_grad.reshape(2 * D, F),
        bias_grad.reshape(F),
    )


def solution(mesh, y_chips=Y_CHIPS):
    dom, feat = mesh.shape["dom"], mesh.shape["feat"]
    sizes = (y_chips, dom // (CORES * y_chips), CORES, feat)
    in_specs = (
        P("dom", "feat"),
        P(None, "feat"),
        P("feat"),
        P("dom", "feat"),
        P("dom", None, None),
        P("dom"),
        P("dom"),
        P("dom"),
        P("dom"),
        P("dom", None),
    )
    out_specs = (P("dom", "feat"), P("dom", "feat"), P(None, "feat"), P("feat"))
    return jax.shard_map(
        functools.partial(per_device, sizes),
        mesh=mesh,
        in_specs=in_specs,
        out_specs=out_specs,
        check_vma=False,
    )
```

time: 863 us -> 112 us (0.13); the launches traced: 852 us -> 112 us
  waiting for transfers between devices: 467 us -> 0 us
  blocking collectives: 249 us -> 0 us
  Pallas kernels: 0 us -> 108 us
  starting transfers between devices: 37.3 us -> 0 us
  local copies, waits for them, and re-layouts: 33.1 us -> 0 us
  matrix products: 32.3 us -> 0 us
  other arithmetic: 18 us -> 2.05 us
  between operations: 15 us -> 1.29 us
    psum x1 -> x0, blocking collectives: 249 us -> none  [per_device(): weight_sum, bias_sum = lax.psum((local_weight, local_bias), 'dom')]
    reduce_scatter x1 -> x0, waiting for transfers between devices: 244 us -> none  [per_device(): lax.psum_scatter(hub_grad, 'dom', scatter_dimension=0, tiled=True)]
    all_gather x4 -> x0, waiting for transfers between devices: 148 us -> none  [the longest x1 96 us: per_device(): hub_table = lax.all_gather(node_feats[hub_rows], 'dom', axis=0, tiled=True)]
    pallas_call x0 -> x2, Pallas kernels: none -> 108 us  [the longest x1 106 us: per_device(): pl.pallas_call(functools.partial(kernel, dims, names), out_shape=[shape f...]
    psum x1 -> x0, waiting for transfers between devices: 51.5 us -> none  [per_device(): weight_sum, bias_sum = lax.psum((local_weight, local_bias), 'dom')]
    all_to_all x4 -> x0, starting transfers between devices: 36.9 us -> none  [the longest x1 20.6 us: per_device(): lax.all_to_all(outgoing, 'dom', split_axis=0, concat_axis=0, tiled=True)]
    dot_general x10 -> x0, matrix products: 32.3 us -> none  [the longest x1 6.47 us: per_device(): jnp.einsum('tij,tjf->tif', tile_values, picked, preferred_element_type=jn...]
    all_to_all x4 -> x0, waiting for transfers between devices: 22.6 us -> none  [the longest x1 13.2 us: per_device(): lax.all_to_all(outgoing, 'dom', split_axis=0, concat_axis=0, tiled=True)]
  transfers between devices with their start and end apart: 10 -> 0, of which waited for: 9 -> 0; matrix products, arithmetic and copies ran while one was open for 9% -> 0% of each run, Pallas kernels for 0% -> 0%
where the time goes in v2:
time: 112 us
  Pallas kernels  108 us (96%)
  other arithmetic  2.05 us (2%)
  between operations  1.29 us (1%)
    pallas_call x1, Pallas kernels, per_device(): pl.pallas_call(functools.partial(kernel, dims, names), out_shape=[shape f...  106 us

profile of v2, /device:TPU:1, one launch (start us, length us, event | category | flops | bytes accessed | tf_op | source)
XLA Modules:
  0.0 111.8 jit_solution(6664633771303720640)
XLA Ops:
  1.3 0.7 compare_select_fusion
  2.0 0.7 select_reduce_fusion.1.refs_7_
  2.7 0.7 select_reduce_fusion.refs_8_
  3.3 106.2 %shard_map.129 = (bf16[4,256,128]{2,1,0:T(8,128)(2,1)}, bf16[1024,128]{1,0:T(8,128)(2,1)}, f32[8,16,8,128]{3,2,1,0:T(8,128)}, f32[1,128]{1,0:T(1,128)}) custom-call(bf16[1024,128]{1,0:T(8,128)(2,1)} %refs_0_.1, bf16[1024,128]{1,0:T(8,128)(2,1)} %refs_1_.1, bf16[1024,128]{1,0:T(8,128)(2,1)} %refs_2_.1, bf16[88,128,128]{2,1,0:T(8,128)(2,1)} %refs_3_.1, ...), custom_call_target="tpu_custom_call" | custom-call | tf_op jit(solution)/shard_map/pallas_call | solution.py:740
  109.6 2.2 %shard_map.130 = (bf16[4,256,128]{2,1,0:T(8,128)(2,1)}, bf16[1024,128]{1,0:T(8,128)(2,1)}, f32[8,16,8,128]{3,2,1,0:T(8,128)}, f32[1,128]{1,0:T(1,128)}) custom-call(bf16[4,256,128]{2,1,0:T(8,128)(2,1)} %get-tuple-element.12.refs_0_, bf16[1024,128]{1,0:T(8,128)(2,1)} %get-tuple-element.13.refs_1_, f32[8,16,8,128]{3,2,1,0:T(8,128)} %get-tuple-element.14.refs_2_, ...), custom_call_target="tpu_custom_call" | custom-call | tf_op jit(solution)/shard_map/pallas_call | solution.py:750

commit v3 on v2

--- a/solution.py
+++ b/solution.py
@@ -32,57 +32,53 @@
         self.size, self.me, self.device = size, me, device
 
     def each(self, body):
-        if self.size <= 4:
-            for step in range(1, self.size):
-                body(step, lax.rem(self.me + step, self.size))
-        else:
-
-            def loop(step, carry):
-                body(step, lax.rem(self.me + step, self.size))
-                return carry
-
-            lax.fori_loop(1, self.size, loop, 0)
+        for step in range(1, self.size):
+            body((self.me + step) & (self.size - 1))
 
 
 class Exchange:
-    def __init__(self, group, src, dst, sems):
+    def __init__(self, group, src, dst, sems, sent, landed, each=False):
         self.group, self.src, self.dst, self.sems = group, src, dst, sems
-
-    def copy(self, step, peer, landing):
+        self.sent, self.landed, self.one_by_one = sent, landed, each
+
+    def copy(self, peer, landing):
         return pltpu.make_async_remote_copy(
             src_ref=self.src(peer),
             dst_ref=self.dst(landing),
-            send_sem=self.sems.at[0, step],
-            recv_sem=self.sems.at[1, landing],
+            send_sem=self.sems.at[0, 0],
+            recv_sem=self.sems.at[1, landing if self.one_by_one else 0],
             device_id=self.group.device(peer),
             device_id_type=pl.DeviceIdType.MESH,
         )
 
+    def all(self, part):
+        return pltpu.make_async_remote_copy(
+            src_ref=part,
+            dst_ref=part,
+            send_sem=self.sems.at[0, 0],
+            recv_sem=self.sems.at[1, 0],
+            device_id=self.group.device((self.group.me + 1) & (self.group.size - 1)),
+            device_id_type=pl.DeviceIdType.MESH,
+        )
+
     def start_to(self, peer):
-        step = lax.rem(peer - self.group.me + self.group.size, self.group.size)
-        self.copy(step, peer, self.group.me).start()
-
-    def start_one(self, step, peer):
-        self.copy(step, peer, self.group.me).start()
+        self.copy(peer, self.group.me).start()
 
     def start(self):
-        self.group.each(self.start_one)
-
-    def wait_one(self, step, peer):
-        self.copy(step, peer, peer).wait_recv()
+        self.group.each(self.start_to)
 
     def wait(self):
-        self.group.each(self.wait_one)
+        self.all(self.landed).wait_recv()
 
     def wait_then(self, after):
-        def body(step, peer):
-            self.wait_one(step, peer)
+        def body(peer):
+            self.copy(peer, peer).wait_recv()
             after(peer)
 
         self.group.each(body)
 
     def drain(self):
-        self.group.each(lambda step, peer: self.copy(step, peer, self.group.me).wait_send())
+        self.all(self.sent).wait_send()
 
 
 class Relay:
@@ -133,15 +129,15 @@
     DY = D // Y
     DZ = DY // Z
     dom, x = lax.axis_index("dom"), lax.axis_index("feat")
-    c = lax.rem(dom, C)
-    z = lax.rem(lax.div(dom, C), Z)
-    y = lax.div(dom, C * Z)
+    c = dom & (C - 1)
+    z = (dom >> log2(C)) & (Z - 1)
+    y = dom >> log2(C * Z)
     yc = y * C + c
 
     def at(yy, zz, cc):
         return ((yy * Z + zz) * C + cc, x)
 
-    gyc = Group(Y * C, yc, lambda p: at(lax.div(p, C), z, lax.rem(p, C)))
+    gyc = Group(Y * C, yc, lambda p: at(p >> log2(C), z, p & (C - 1)))
     gz = Group(Z, z, lambda p: at(y, p, c))
     gy = Group(Y, y, lambda p: at(p, z, c))
     gc = Group(C, c, lambda p: at(y, z, p))
@@ -151,7 +147,7 @@
     barrier = pltpu.get_barrier_semaphore()
     for group in (gyc, gz, gx):
         group.each(
-            lambda step, peer, group=group: pl.semaphore_signal(
+            lambda peer, group=group: pl.semaphore_signal(
                 barrier, inc=1, device_id=group.device(peer), device_id_type=pl.DeviceIdType.MESH
             )
         )
@@ -225,14 +221,31 @@
 
     done = []
 
-    def exchange(group, src, dst, sems):
-        ex = Exchange(group, src, dst, sems)
+    def most(ref):
+        return ref.at[pl.ds(0, ref.shape[0] - 1)]
+
+    def cols3(ref):
+        return ref.at[:, 0 : D - F]
+
+
+    def exchange(group, src, dst, sems, sent, landed, each=False):
+        ex = Exchange(group, src, dst, sems, sent, landed, each)
         done.append(ex)
         return ex
 
-    ex_yc = exchange(gyc, lambda p: r.out_halo.at[p], lambda p: r.st1.at[p], r.s_yc)
+    ex_yc = exchange(
+        gyc, lambda p: r.out_halo.at[p], lambda p: r.st1.at[p],
+        r.s_yc,
+        most(r.out_halo),
+        most(r.st1),
+    )
     ex_yc.start()
-    ex_hz = exchange(gz, lambda p: r.hub.at[y, z, c], lambda p: r.hub.at[y, p, c], r.s_hz)
+    ex_hz = exchange(
+        gz, lambda p: r.hub.at[y, z, c], lambda p: r.hub.at[y, p, c],
+        r.s_hz,
+        r.hub.at[y, pl.ds(0, Z - 1), c],
+        r.hub.at[y, pl.ds(0, Z - 1), c],
+    )
     ex_hz.start()
     r.st1[yc] = r.out_halo[yc]
 
@@ -240,17 +253,32 @@
     fetch_w.wait()
     fetch_og.wait()
     ex_xw = exchange(
-        gx, lambda p: r.wv.at[wrows], lambda p: r.wfull.at[wrows, cols_of(p)], r.s_xw
+        gx, lambda p: r.wv.at[wrows], lambda p: r.wfull.at[wrows, cols_of(p)],
+        r.s_xw,
+        r.wfull.at[wrows, 0 : D - F],
+        r.wfull.at[wrows, 0 : D - F],
+        each=True,
     )
     ex_xw.start()
     ex_xs = exchange(
-        gx, lambda p: r.nf.at[rows_of(p)], lambda p: r.selfc.at[:, cols_of(p)], r.s_xs
+        gx, lambda p: r.nf.at[rows_of(p)], lambda p: r.selfc.at[:, cols_of(p)],
+        r.s_xs,
+        cols3(r.selfc),
+        cols3(r.selfc),
     )
     ex_xs.start()
-    ex_xb = exchange(gx, lambda p: r.bias8, lambda p: r.biasc.at[:, cols_of(p)], r.s_xb)
+    ex_xb = exchange(
+        gx, lambda p: r.bias8, lambda p: r.biasc.at[:, cols_of(p)],
+        r.s_xb,
+        cols3(r.biasc),
+        cols3(r.biasc),
+    )
     ex_xb.start()
     ex_xo = exchange(
-        gx, lambda p: r.ogv.at[rows_of(p)], lambda p: r.ogc.at[:, cols_of(p)], r.s_xo
+        gx, lambda p: r.ogv.at[rows_of(p)], lambda p: r.ogc.at[:, cols_of(p)],
+        r.s_xo,
+        cols3(r.ogc),
+        cols3(r.ogc),
     )
     ex_xo.start()
     r.biasc[:, cols_of(x)] = r.bias8[...]
@@ -259,13 +287,19 @@
     r.wfull[:, cols_of(x)] = r.wv[...]
 
     fetch_tiles.wait()
-    r.acc_tiles[0] = jnp.zeros((T, T), BF16)
+    turn = NT // 8 if NT % 8 == 0 else 1
+
+    def turn_tiles(i, carry):
+        for k in range(NT // turn):
+            t = i * (NT // turn) + k
+            r.turned[t] = r.tile_buf[t].T
+        return carry
+
+    lax.fori_loop(0, turn, turn_tiles, 0)
     r.acc_tiles_t[0] = jnp.zeros((T, T), BF16)
 
     def add_tile(t, carry):
-        value = r.tile_buf[t].astype(F32) + r.acc_tiles[r.prev[t]].astype(F32)
-        r.acc_tiles[t + 1] = value.astype(BF16)
-        r.acc_tiles_t[t + 1] = value.T.astype(BF16)
+        r.acc_tiles_t[t + 1] = r.turned[t] + r.acc_tiles_t[r.prev[t]]
         return carry
 
     lax.fori_loop(0, NT, add_tile, 0)
@@ -274,21 +308,23 @@
     r.halo_z[...] = (
         dot(perm(z_major), r.st1[...].reshape(HALO, F)).astype(BF16).reshape(Z, YCC, F)
     )
-    ex_z = exchange(gz, lambda p: r.halo_z.at[p], lambda p: r.st2.at[p], r.s_z)
+    ex_z = exchange(
+        gz, lambda p: r.halo_z.at[p], lambda p: r.st2.at[p],
+        r.s_z,
+        most(r.halo_z),
+        most(r.st2),
+    )
     ex_z.start()
     r.st2[z] = r.halo_z[z]
 
-    def place(s, carry):
-        for n in range(NB):
-            slot = r.last[n * SB + s]
-            r.adj[n * T : (n + 1) * T, aligned(s * T, T)] = r.acc_tiles[slot]
-            r.adj_t[aligned(s * T, T), n * T : (n + 1) * T] = r.acc_tiles_t[slot]
-        return carry
-
-    lax.fori_loop(0, SB, place, 0)
-
     ex_hz.wait()
-    ex_hy = exchange(gy, lambda p: r.hub.at[y, :, c], lambda p: r.hub.at[p, :, c], r.s_hy)
+    ex_hy = exchange(
+        gy, lambda p: r.hub.at[y, :, c], lambda p: r.hub.at[p, :, c],
+        r.s_hy,
+        r.hub.at[pl.ds(0, Y - 1), :, c],
+        r.hub.at[pl.ds(0, Y - 1), :, c],
+        each=True,
+    )
     ex_hy.start()
     hub_to = Relay(other_core, r.s_hc, lambda p: r.hub.at[p, :, c], lambda p: r.hub.at[p, :, c])
     hub_from = Relay(
@@ -309,22 +345,22 @@
         lambda p: r.wfull.at[other_rows, cols_of(p)],
         lambda p: r.wfull.at[other_rows, cols_of(p)],
     )
-    def add_deg(n, carry):
-        rows = aligned(n * T, T)
-        lanes = r.adj[rows, 0:T]
-        for s in range(1, SB):
-            lanes = lanes + r.adj[rows, s * T : (s + 1) * T]
-        r.deg[rows, :] = 1.0 / jnp.maximum(dot(lanes, ones), 1.0)
+    def place(s, carry):
+        for n in range(NB):
+            r.adj_t[aligned(s * T, T), n * T : (n + 1) * T] = r.acc_tiles_t[r.last[n * SB + s]]
         return carry
 
-    ones = jnp.ones((T, F), BF16)
-    lax.fori_loop(0, NB, add_deg, 0)
-    r.acc[...] = dot(r.adj[:, 0:N], r.nf[...])
+    lax.fori_loop(0, SB, place, 0)
+
+    def gather(rows, source):
+        ones = jnp.ones((16, source.shape[0]), BF16)
+        return dot(jnp.concatenate([source.T, ones], axis=0), r.adj_t[rows, :])
 
     def add_hub(p):
-        cols = pl.ds(pl.multiple_of(N + HALO + p * PERY, T), PERY)
-        r.acc[...] += dot(r.adj[:, cols], r.hub[p].reshape(PERY, F))
-
+        rows = pl.ds(pl.multiple_of(N + HALO + p * PERY, T), PERY)
+        r.acc[...] += gather(rows, r.hub[p].reshape(PERY, F))
+
+    r.acc[...] = gather(slice(0, N), r.nf[...])
     hub_from.copy(y).wait_recv()
     add_hub(y)
 
@@ -333,15 +369,19 @@
 
     ex_z.wait()
     halo = dot(perm(to_dom), r.st2[...].reshape(HALO, F)).astype(BF16)
-    r.acc[...] += dot(r.adj[:, N : N + HALO], halo)
+    r.acc[...] += gather(slice(N, N + HALO), halo)
 
     for i in range(1, Y):
-        p = lax.rem(y + i, Y)
+        p = (y + i) & (Y - 1)
         hub_from.copy(p).wait_recv()
         add_hub(p)
-    r.mean[...] = (r.acc[...] * r.deg[...]).astype(BF16)
+    r.inv[...] = 1.0 / jnp.maximum(r.acc[F : F + 8, :], 1.0)
+    r.mean[...] = (r.acc[0:F, :] * r.inv[0:1, :]).astype(BF16).T
     ex_xm = exchange(
-        gx, lambda p: r.mean.at[rows_of(p)], lambda p: r.meanc.at[:, cols_of(p)], r.s_xm
+        gx, lambda p: r.mean.at[rows_of(p)], lambda p: r.meanc.at[:, cols_of(p)],
+        r.s_xm,
+        cols3(r.meanc),
+        cols3(r.meanc),
     )
     ex_xm.start()
     r.meanc[:, cols_of(x)] = r.mean[rows_of(x), :]
@@ -349,7 +389,7 @@
     ex_xs.wait()
     ex_xb.wait()
     ex_xo.wait()
-    gx.each(lambda step, peer: w_from.copy(peer).wait_recv())
+    gx.each(lambda peer: w_from.copy(peer).wait_recv())
     r.pre[...] = dot(r.selfc[...], r.wfull[0:D, :]) + r.biasc[0:1, :]
 
     for k in range(CUT):
@@ -358,16 +398,21 @@
             row == lax.broadcasted_iota(jnp.int32, (N, DOM), 0)
         ).astype(BF16)
 
+    inv_rows = jnp.broadcast_to(r.inv[0:1, rows_of(x)], (F, R)).T
     ex_xm.wait()
     pre_act = r.pre[...] + dot(r.meanc[...], r.wfull[D : 2 * D, :])
     sig = jax.nn.sigmoid(pre_act)
     r.gp[...] = (r.ogc[...].astype(F32) * (sig * (1.0 + pre_act * (1.0 - sig)))).astype(BF16)
     r.lo_send[...] = (pre_act * sig).astype(BF16)
-    inv_rows = r.deg[rows_of(x), :]
     cat_mean = dot_nt(r.gp[...], r.wfull[D : 2 * D, :])
     for j in range(X):
         r.gm_send[j] = (cat_mean[:, j * F : (j + 1) * F] * inv_rows).astype(BF16)
-    ex_xg = exchange(gx, lambda p: r.gm_send.at[p], lambda p: r.gm.at[p], r.s_xg)
+    ex_xg = exchange(
+        gx, lambda p: r.gm_send.at[p], lambda p: r.gm.at[p],
+        r.s_xg,
+        most(r.gm_send),
+        most(r.gm),
+    )
     ex_xg.start()
     r.gm[x] = r.gm_send[x]
 
@@ -376,7 +421,12 @@
             part = dot_tn(src[:, q : q + 2 * T], r.gp[...])
             r.wg32[half, q : q + 2 * T, :] = part
             r.wgb[half, q : q + 2 * T, :] = part.astype(BF16)
-    ex_gc = exchange(gc, lambda p: r.wgb.at[p], lambda p: r.wg_core.at[p], r.s_gc)
+    ex_gc = exchange(
+        gc, lambda p: r.wgb.at[p], lambda p: r.wg_core.at[p],
+        r.s_gc,
+        most(r.wgb),
+        most(r.wg_core),
+    )
     ex_gc.start()
     bias_sum = jnp.sum(r.gp[...].astype(F32), axis=0, keepdims=True)
 
@@ -400,13 +450,26 @@
         r.wx_send[j, 0:D, :] = block.astype(BF16)
         r.wx_own[j, D : D + 8, :] = jnp.broadcast_to(bias_sum[:, cols], (8, F))
         r.wx_send[j, D : D + 16, :] = bias_rows(bias_sum[:, cols])
-    ex_gx = exchange(gx, lambda p: r.wx_send.at[p], lambda p: r.wx_recv.at[p], r.s_gx)
+    ex_gx = exchange(
+        gx, lambda p: r.wx_send.at[p], lambda p: r.wx_recv.at[p],
+        r.s_gx,
+        most(r.wx_send),
+        most(r.wx_recv),
+    )
     ex_gx.start()
 
-    ex_xgs = exchange(gx, lambda p: r.gs_send.at[p], lambda p: r.gs_recv.at[p], r.s_xgs)
+    ex_xgs = exchange(
+        gx, lambda p: r.gs_send.at[p], lambda p: r.gs_recv.at[p],
+        r.s_xgs,
+        most(r.gs_send),
+        most(r.gs_recv),
+    )
     ex_xgs.start()
     ex_xl = exchange(
-        gx, lambda p: r.lo_send.at[:, cols_of(p)], lambda p: r.lo_recv.at[p], r.s_xl
+        gx, lambda p: r.lo_send.at[:, cols_of(p)], lambda p: r.lo_recv.at[p],
+        r.s_xl,
+        cols3(r.lo_send),
+        most(r.lo_recv),
     )
     ex_xl.start()
     r.lo_recv[x] = r.lo_send[:, cols_of(x)]
@@ -416,7 +479,12 @@
     core_to = Relay(
         other_core, r.s_bhc, lambda p: r.hsb.at[1 - c, p], lambda p: r.hs_core.at[p]
     )
-    ex_bhy = exchange(gy, lambda p: r.hy_send.at[p], lambda p: r.hy_recv.at[p], r.s_bhy)
+    ex_bhy = exchange(
+        gy, lambda p: r.hy_send.at[p], lambda p: r.hy_recv.at[p],
+        r.s_bhy,
+        most(r.hy_send),
+        most(r.hy_recv),
+    )
 
     def spread(rows):
         return dot(r.adj_t[rows, :], r.gm[...].reshape(N, F))
@@ -437,7 +505,7 @@
             r.hy_send[p] = pair.astype(BF16)
             ex_bhy.start_to(p)
 
-    order = [lax.rem(y + i, Y) for i in range(1, Y)] + [y]
+    order = [(y + i) & (Y - 1) for i in range(1, Y)] + [y]
     back_hub(order[0])
     for i in range(1, Y):
         back_hub(order[i])
@@ -445,7 +513,12 @@
 
     halo_b = spread(slice(N, N + HALO)).astype(BF16)
     r.halo_zb[...] = dot(perm(from_dom), halo_b).astype(BF16).reshape(Z, YCC, F)
-    ex_rz = exchange(gz, lambda p: r.halo_zb.at[p], lambda p: r.rt1.at[p], r.s_rz)
+    ex_rz = exchange(
+        gz, lambda p: r.halo_zb.at[p], lambda p: r.rt1.at[p],
+        r.s_rz,
+        most(r.halo_zb),
+        most(r.rt1),
+    )
     ex_rz.start()
     r.rt1[z] = r.halo_zb[z]
 
@@ -463,7 +536,12 @@
         r.wy_own[j] = block
         r.wy_send[j, 0:DY, :] = block.astype(BF16)
         r.wy_send[j, DY : DY + 16, :] = bias_rows(bsum[0:1])
-    ex_gy = exchange(gy, lambda p: r.wy_send.at[p], lambda p: r.wy_recv.at[p], r.s_gy)
+    ex_gy = exchange(
+        gy, lambda p: r.wy_send.at[p], lambda p: r.wy_recv.at[p],
+        r.s_gy,
+        most(r.wy_send),
+        most(r.wy_recv),
+    )
     ex_gy.start()
 
     r.total[...] = spread(slice(0, N))
@@ -471,24 +549,6 @@
     ex_xgs.wait()
     for j in range(X):
         r.total[j * R : (j + 1) * R, :] += r.gs_recv[j].astype(F32)
-
-    r.hy_recv[y] = jnp.zeros((Z, HD, F), BF16)
-    ex_bhy.wait()
-    hub_y = r.hy_own[...]
-    for p in range(Y):
-        hub_y = hub_y + r.hy_recv[p].astype(F32)
-    r.hy_own[...] = hub_y
-    r.hz_send[...] = hub_y.astype(BF16)
-    ex_bhz = exchange(gz, lambda p: r.hz_send.at[p], lambda p: r.hz_recv.at[p], r.s_bhz)
-    ex_bhz.start()
-
-    ex_rz.wait()
-    r.halo_m[...] = (
-        dot(perm(yc_major), r.rt1[...].reshape(HALO, F)).astype(BF16).reshape(Y * C, ZC, F)
-    )
-    ex_ryc = exchange(gyc, lambda p: r.halo_m.at[p], lambda p: r.rt2.at[p], r.s_ryc)
-    ex_ryc.start()
-    r.rt2[yc] = r.halo_m[yc]
 
     r.wy_recv[y] = jnp.zeros((DY + 16, F), BF16)
     ex_gy.wait()
@@ -499,26 +559,69 @@
     for j in range(Z):
         r.wz_send[j, 0:DZ, :] = wsum[j * DZ : (j + 1) * DZ]
         r.wz_send[j, DZ : DZ + 8, :] = bsum
-    ex_gz = exchange(gz, lambda p: r.wz_send.at[p], lambda p: r.wz_recv.at[p], r.s_gz)
+    ex_gz = exchange(
+        gz, lambda p: r.wz_send.at[p], lambda p: r.wz_recv.at[p],
+        r.s_gz,
+        most(r.wz_send),
+        most(r.wz_recv),
+    )
     ex_gz.start()
 
-    ex_xl.wait()
-    lo_out = local(5, r.lo_recv, r.layer_out)
-    lo_out.start()
-
-    ex_ryc.wait()
-    returned = dot(perm(from_peer_major(dims)), r.rt2[...].reshape(HALO, F)).astype(BF16)
-    r.total[...] += dot(r.hot_t[...], returned)
+    r.hy_recv[y] = jnp.zeros((Z, HD, F), BF16)
+    ex_bhy.wait()
+    hub_y = r.hy_own[...]
+    for p in range(Y):
+        hub_y = hub_y + r.hy_recv[p].astype(F32)
+    r.hy_own[...] = hub_y
+    r.hz_send[...] = hub_y.astype(BF16)
+    ex_bhz = exchange(
+        gz, lambda p: r.hz_send.at[p], lambda p: r.hz_recv.at[p],
+        r.s_bhz,
+        most(r.hz_send),
+        most(r.hz_recv),
+    )
+    ex_bhz.start()
+
+    ex_rz.wait()
+    r.halo_m[...] = (
+        dot(perm(yc_major), r.rt1[...].reshape(HALO, F)).astype(BF16).reshape(Y * C, ZC, F)
+    )
+    ex_ryc = exchange(
+        gyc, lambda p: r.halo_m.at[p], lambda p: r.rt2.at[p],
+        r.s_ryc,
+        most(r.halo_m),
+        most(r.rt2),
+    )
+    ex_ryc.start()
+    r.rt2[yc] = r.halo_m[yc]
 
     r.wz_recv[z] = jnp.zeros((DZ + 8, F), F32)
     ex_gz.wait()
     zsum = (jnp.sum(r.wz_recv[...], axis=0) + r.wz_send[z]) * scale
     r.wout[z] = zsum[0:DZ]
     r.bias_core[c] = zsum[DZ : DZ + 8]
-    ex_az = exchange(gz, lambda p: r.wout.at[z], lambda p: r.wout.at[p], r.s_az)
+    ex_az = exchange(
+        gz, lambda p: r.wout.at[z], lambda p: r.wout.at[p],
+        r.s_az,
+        most(r.wout),
+        most(r.wout),
+    )
     ex_az.start()
-    ex_bc = exchange(gc, lambda p: r.bias_core.at[c], lambda p: r.bias_core.at[p], r.s_bc)
+    ex_bc = exchange(
+        gc, lambda p: r.bias_core.at[c], lambda p: r.bias_core.at[p],
+        r.s_bc,
+        most(r.bias_core),
+        most(r.bias_core),
+    )
     ex_bc.start()
+
+    ex_xl.wait()
+    lo_out = local(5, r.lo_recv, r.layer_out)
+    lo_out.start()
+
+    ex_ryc.wait()
+    returned = dot(perm(from_peer_major(dims)), r.rt2[...].reshape(HALO, F)).astype(BF16)
+    r.total[...] += dot(r.hot_t[...], returned)
 
     r.hz_recv[z] = jnp.zeros((HD, F), BF16)
     ex_bhz.wait()
@@ -537,8 +640,10 @@
     ex_ay = exchange(
         gyc,
         lambda p: r.wb_all.at[yc_row(c, Y, y)],
-        lambda p: r.wb_all.at[yc_row(lax.rem(p, C), Y, lax.div(p, C))],
+        lambda p: r.wb_all.at[yc_row(p & (C - 1), Y, p >> log2(C))],
         r.s_ay,
+        most(r.wb_all),
+        most(r.wb_all),
     )
     ex_ay.start()
     ex_bc.wait()
@@ -557,7 +662,7 @@
     for p in range(Y):
         hub_to.copy(p).wait_send()
         core_to.copy(p).wait_send()
-    gx.each(lambda step, peer: w_to.copy(peer).wait_send())
+    gx.each(lambda peer: w_to.copy(peer).wait_send())
 
 
 def yc_row(c, Y, y):
@@ -649,9 +754,8 @@
     scratch = dict(
         nf=b(N, F),
         tile_buf=b(NT, T, T),
-        acc_tiles=b(NT + 1, T, T),
+        turned=b(NT, T, T),
         acc_tiles_t=b(NT + 1, T, T),
-        adj=b(N, SB * T),
         adj_t=b(SB * T, N),
         hot=b(HALO, N),
         hot_t=b(N, HALO),
@@ -660,8 +764,8 @@
         st2=b(Z, YCC, F),
         halo_z=b(Z, YCC, F),
         hub=b(Y, Z, C, HD, F),
-        deg=f(N, F),
-        acc=f(N, F),
+        acc=f(F + 16, N),
+        inv=f(8, N),
         selfc=b(R, D),
         meanc=b(R, D),
         ogc=b(R, D),

time: 112 us -> 98.4 us (0.88)
  Pallas kernels: 108 us -> 94.8 us
    pallas_call x1, Pallas kernels: 106 us -> 92.6 us  [per_device(): pl.pallas_call(functools.partial(kernel, dims, names), out_shape=[shape f...]
where the time goes in v3:
time: 98.4 us; the launch traced here: 98.2 us
  Pallas kernels  94.8 us (96%)
  other arithmetic  2.05 us (2%)
  between operations  1.29 us (1%)
    pallas_call x1, Pallas kernels, per_device(): pl.pallas_call(functools.partial(kernel, dims, names), out_shape=[shape f...  92.6 us
    pallas_call x1, Pallas kernels, per_device(): pl.pallas_call(copy_kernel, out_shape=[jax.ShapeDtypeStruct(v.shape, v.dt...  2.19 us

profile of v3, /device:TPU:1, one launch (start us, length us, event | category | flops | bytes accessed | tf_op | source)
XLA Modules:
  0.0 98.2 jit_solution(13039125878986594302)
XLA Ops:
  1.3 0.7 compare_select_fusion
  2.0 0.7 select_reduce_fusion.1.refs_7_
  2.7 0.7 select_reduce_fusion.refs_8_
  3.3 92.6 %shard_map.129 = (bf16[4,256,128]{2,1,0:T(8,128)(2,1)}, bf16[1024,128]{1,0:T(8,128)(2,1)}, f32[8,16,8,128]{3,2,1,0:T(8,128)}, f32[1,128]{1,0:T(1,128)}) custom-call(bf16[1024,128]{1,0:T(8,128)(2,1)} %refs_0_.1, bf16[1024,128]{1,0:T(8,128)(2,1)} %refs_1_.1, bf16[1024,128]{1,0:T(8,128)(2,1)} %refs_2_.1, bf16[88,128,128]{2,1,0:T(8,128)(2,1)} %refs_3_.1, ...), custom_call_target="tpu_custom_call" | custom-call | tf_op jit(solution)/shard_map/pallas_call | solution.py:844
  96.0 2.2 %shard_map.130 = (bf16[4,256,128]{2,1,0:T(8,128)(2,1)}, bf16[1024,128]{1,0:T(8,128)(2,1)}, f32[8,16,8,128]{3,2,1,0:T(8,128)}, f32[1,128]{1,0:T(1,128)}) custom-call(bf16[4,256,128]{2,1,0:T(8,128)(2,1)} %get-tuple-element.12.refs_0_, bf16[1024,128]{1,0:T(8,128)(2,1)} %get-tuple-element.13.refs_1_, f32[8,16,8,128]{3,2,1,0:T(8,128)} %get-tuple-element.14.refs_2_, ...), custom_call_target="tpu_custom_call" | custom-call | tf_op jit(solution)/shard_map/pallas_call | solution.py:854

commit v4 on v3

--- a/solution.py
+++ b/solution.py
@@ -68,6 +68,8 @@
         self.group.each(self.start_to)
 
     def wait(self):
+        if self.group.size == 1:
+            return
         self.all(self.landed).wait_recv()
 
     def wait_then(self, after):
@@ -78,6 +80,8 @@
         self.group.each(body)
 
     def drain(self):
+        if self.group.size == 1:
+            return
         self.all(self.sent).wait_send()
 
 
@@ -127,7 +131,9 @@
     ZC, YCC = Z * CUT, Y * C * CUT
     PERY = Z * C * HD
     DY = D // Y
-    DZ = DY // Z
+    RES = Z // 4 if Z >= 8 else Z
+    ZQ = Z // RES
+    DN = DY // RES
     dom, x = lax.axis_index("dom"), lax.axis_index("feat")
     c = dom & (C - 1)
     z = (dom >> log2(C)) & (Z - 1)
@@ -140,6 +146,15 @@
     gyc = Group(Y * C, yc, lambda p: at(p >> log2(C), z, p & (C - 1)))
     gz = Group(Z, z, lambda p: at(y, p, c))
     gy = Group(Y, y, lambda p: at(p, z, c))
+    zr, zq = z & (RES - 1), z >> log2(RES)
+
+    def near(p):
+        step = (p - zr) & (RES - 1)
+        step = jnp.where(step > RES // 2, step - RES, step)
+        return at(y, (z + step) & (Z - 1), c)
+
+    gfar = Group(Z // RES, zq, lambda p: at(y, (p << log2(RES)) | zr, c))
+    gnear = Group(RES, zr, near)
     gc = Group(C, c, lambda p: at(y, z, p))
     gx = Group(X, x, lambda p: (dom, p))
     other_core = at(y, z, 1 - c)
@@ -213,7 +228,7 @@
         return (yy * Z + zz) * (C * CUT) + mod_(i, C * CUT)
 
     fetch_nf.wait()
-    r.hub[y, z, c] = dot(hub_hot, r.nf[...]).astype(BF16)
+    r.hub[y, zq, zr, c] = dot(hub_hot, r.nf[...]).astype(BF16)
     picked = dot(r.hot[...], r.nf[...]).astype(BF16)
     r.out_halo[...] = dot(perm(peer_major), picked).astype(BF16).reshape(Y * C, ZC, F)
     r.bias8[...] = jnp.broadcast_to(r.bias[...], (8, F))
@@ -241,10 +256,12 @@
     )
     ex_yc.start()
     ex_hz = exchange(
-        gz, lambda p: r.hub.at[y, z, c], lambda p: r.hub.at[y, p, c],
+        gfar,
+        lambda p: r.hub.at[y, zq, zr, c],
+        lambda p: r.hub.at[y, p, zr, c],
         r.s_hz,
-        r.hub.at[y, pl.ds(0, Z - 1), c],
-        r.hub.at[y, pl.ds(0, Z - 1), c],
+        r.hub.at[y, pl.ds(0, ZQ - 1), zr, c],
+        r.hub.at[y, pl.ds(0, ZQ - 1), zr, c],
     )
     ex_hz.start()
     r.st1[yc] = r.out_halo[yc]
@@ -298,6 +315,17 @@
     lax.fori_loop(0, turn, turn_tiles, 0)
     r.acc_tiles_t[0] = jnp.zeros((T, T), BF16)
 
+    ex_hz.wait()
+    ex_hn = exchange(
+        gnear,
+        lambda p: r.hub.at[y, :, zr, c],
+        lambda p: r.hub.at[y, :, p, c],
+        r.s_hn,
+        r.hub.at[y, :, pl.ds(0, RES - 1), c],
+        r.hub.at[y, :, pl.ds(0, RES - 1), c],
+    )
+    ex_hn.start()
+
     def add_tile(t, carry):
         r.acc_tiles_t[t + 1] = r.turned[t] + r.acc_tiles_t[r.prev[t]]
         return carry
@@ -317,18 +345,18 @@
     ex_z.start()
     r.st2[z] = r.halo_z[z]
 
-    ex_hz.wait()
+    ex_hn.wait()
     ex_hy = exchange(
-        gy, lambda p: r.hub.at[y, :, c], lambda p: r.hub.at[p, :, c],
+        gy, lambda p: r.hub.at[y, :, :, c], lambda p: r.hub.at[p, :, :, c],
         r.s_hy,
-        r.hub.at[pl.ds(0, Y - 1), :, c],
-        r.hub.at[pl.ds(0, Y - 1), :, c],
+        r.hub.at[pl.ds(0, Y - 1), :, :, c],
+        r.hub.at[pl.ds(0, Y - 1), :, :, c],
         each=True,
     )
     ex_hy.start()
-    hub_to = Relay(other_core, r.s_hc, lambda p: r.hub.at[p, :, c], lambda p: r.hub.at[p, :, c])
+    hub_to = Relay(other_core, r.s_hc, lambda p: r.hub.at[p, :, :, c], lambda p: r.hub.at[p, :, :, c])
     hub_from = Relay(
-        other_core, r.s_hc, lambda p: r.hub.at[p, :, 1 - c], lambda p: r.hub.at[p, :, 1 - c]
+        other_core, r.s_hc, lambda p: r.hub.at[p, :, :, 1 - c], lambda p: r.hub.at[p, :, :, 1 - c]
     )
     hub_to.start(y)
 
@@ -457,23 +485,6 @@
         most(r.wx_recv),
     )
     ex_gx.start()
-
-    ex_xgs = exchange(
-        gx, lambda p: r.gs_send.at[p], lambda p: r.gs_recv.at[p],
-        r.s_xgs,
-        most(r.gs_send),
-        most(r.gs_recv),
-    )
-    ex_xgs.start()
-    ex_xl = exchange(
-        gx, lambda p: r.lo_send.at[:, cols_of(p)], lambda p: r.lo_recv.at[p],
-        r.s_xl,
-        cols3(r.lo_send),
-        most(r.lo_recv),
-    )
-    ex_xl.start()
-    r.lo_recv[x] = r.lo_send[:, cols_of(x)]
-    r.gs_recv[x] = r.gs_send[x]
 
     ex_xg.wait()
     core_to = Relay(
@@ -544,11 +555,24 @@
     )
     ex_gy.start()
 
+    ex_xgs = exchange(
+        gx, lambda p: r.gs_send.at[p], lambda p: r.gs_recv.at[p],
+        r.s_xgs,
+        most(r.gs_send),
+        most(r.gs_recv),
+    )
+    ex_xgs.start()
+    ex_xl = exchange(
+        gx, lambda p: r.lo_send.at[:, cols_of(p)], lambda p: r.lo_recv.at[p],
+        r.s_xl,
+        cols3(r.lo_send),
+        most(r.lo_recv),
+    )
+    ex_xl.start()
+    r.lo_recv[x] = r.lo_send[:, cols_of(x)]
+    r.gs_recv[x] = r.gs_send[x]
+
     r.total[...] = spread(slice(0, N))
-
-    ex_xgs.wait()
-    for j in range(X):
-        r.total[j * R : (j + 1) * R, :] += r.gs_recv[j].astype(F32)
 
     r.wy_recv[y] = jnp.zeros((DY + 16, F), BF16)
     ex_gy.wait()
@@ -556,31 +580,57 @@
     for j in range(Y):
         wsum = wsum + r.wy_recv[j, 0:DY, :].astype(F32)
         bsum = bsum + bias_of(r.wy_recv[j, DY : DY + 16, :])
-    for j in range(Z):
-        r.wz_send[j, 0:DZ, :] = wsum[j * DZ : (j + 1) * DZ]
-        r.wz_send[j, DZ : DZ + 8, :] = bsum
-    ex_gz = exchange(
-        gz, lambda p: r.wz_send.at[p], lambda p: r.wz_recv.at[p],
-        r.s_gz,
-        most(r.wz_send),
-        most(r.wz_recv),
-    )
-    ex_gz.start()
+    for p in range(RES):
+        block = wsum[p * DN : (p + 1) * DN]
+        r.wn_own[p] = block
+        r.wn_send[p, 0:DN, :] = block.astype(BF16)
+        r.wn_send[p, DN : DN + 16, :] = bias_rows(bsum[0:1])
+    ex_gn = exchange(
+        gnear,
+        lambda p: r.wn_send.at[p],
+        lambda p: r.wn_recv.at[p],
+        r.s_gn,
+        most(r.wn_send),
+        most(r.wn_recv),
+    )
+    ex_gn.start()
 
     r.hy_recv[y] = jnp.zeros((Z, HD, F), BF16)
     ex_bhy.wait()
     hub_y = r.hy_own[...]
     for p in range(Y):
         hub_y = hub_y + r.hy_recv[p].astype(F32)
-    r.hy_own[...] = hub_y
-    r.hz_send[...] = hub_y.astype(BF16)
-    ex_bhz = exchange(
-        gz, lambda p: r.hz_send.at[p], lambda p: r.hz_recv.at[p],
-        r.s_bhz,
+    hub_y = hub_y.reshape(ZQ, RES, HD, F)
+    for p in range(RES):
+        r.hz_own[p] = hub_y[:, p]
+        r.hz_send[p] = hub_y[:, p].astype(BF16)
+    ex_bhn = exchange(
+        gnear,
+        lambda p: r.hz_send.at[p],
+        lambda p: r.hz_recv.at[p],
+        r.s_bhn,
         most(r.hz_send),
         most(r.hz_recv),
     )
-    ex_bhz.start()
+    ex_bhn.start()
+
+    r.wn_recv[zr] = jnp.zeros((DN + 16, F), BF16)
+    ex_gn.wait()
+    wsum = r.wn_own[zr]
+    for p in range(RES):
+        wsum = wsum + r.wn_recv[p, 0:DN, :].astype(F32)
+        bsum = bsum + bias_of(r.wn_recv[p, DN : DN + 16, :])
+    r.wf_all[zq, 0:DN, :] = wsum.astype(BF16)
+    r.wf_all[zq, DN : DN + 16, :] = bias_rows(bsum[0:1])
+    ex_gf = exchange(
+        gfar,
+        lambda p: r.wf_all.at[zq],
+        lambda p: r.wf_all.at[p],
+        r.s_gf,
+        most(r.wf_all),
+        most(r.wf_all),
+    )
+    ex_gf.start()
 
     ex_rz.wait()
     r.halo_m[...] = (
@@ -595,16 +645,30 @@
     ex_ryc.start()
     r.rt2[yc] = r.halo_m[yc]
 
-    r.wz_recv[z] = jnp.zeros((DZ + 8, F), F32)
-    ex_gz.wait()
-    zsum = (jnp.sum(r.wz_recv[...], axis=0) + r.wz_send[z]) * scale
-    r.wout[z] = zsum[0:DZ]
-    r.bias_core[c] = zsum[DZ : DZ + 8]
+    r.hz_recv[zr] = jnp.zeros((ZQ, HD, F), BF16)
+    ex_bhn.wait()
+    hub_z = r.hz_own[zr] + jnp.sum(r.hz_recv[...].astype(F32), axis=0)
+    r.hf_own[...] = hub_z
+    r.hf_send[...] = hub_z.astype(BF16)
+    ex_bhf = exchange(
+        gfar,
+        lambda p: r.hf_send.at[p],
+        lambda p: r.hf_recv.at[p],
+        r.s_bhf,
+        most(r.hf_send),
+        most(r.hf_recv),
+    )
+    ex_bhf.start()
+
+    ex_gf.wait()
+    for q in range(ZQ):
+        far = r.wf_all[q].astype(F32)
+        wtotal = far[0:DN] if q == 0 else wtotal + far[0:DN]
+        btotal = bias_of(far[DN : DN + 16]) + (0.0 if q == 0 else btotal)
+    r.wa[zr] = (wtotal * scale).astype(BF16)
+    r.bias_core[c] = btotal * scale
     ex_az = exchange(
-        gz, lambda p: r.wout.at[z], lambda p: r.wout.at[p],
-        r.s_az,
-        most(r.wout),
-        most(r.wout),
+        gnear, lambda p: r.wa.at[zr], lambda p: r.wa.at[p], r.s_az, most(r.wa), most(r.wa)
     )
     ex_az.start()
     ex_bc = exchange(
@@ -615,17 +679,29 @@
     )
     ex_bc.start()
 
-    ex_xl.wait()
-    lo_out = local(5, r.lo_recv, r.layer_out)
-    lo_out.start()
+    ex_xgs.wait()
+    for j in range(X):
+        r.total[j * R : (j + 1) * R, :] += r.gs_recv[j].astype(F32)
 
     ex_ryc.wait()
     returned = dot(perm(from_peer_major(dims)), r.rt2[...].reshape(HALO, F)).astype(BF16)
     r.total[...] += dot(r.hot_t[...], returned)
 
-    r.hz_recv[z] = jnp.zeros((HD, F), BF16)
-    ex_bhz.wait()
-    hub_mine = r.hy_own[z] + jnp.sum(r.hz_recv[...].astype(F32), axis=0)
+    ex_az.wait()
+    r.wb_all[yc_row(c, Y, y)] = r.wa[...].reshape(DY, F)
+    ex_ay = exchange(
+        gyc,
+        lambda p: r.wb_all.at[yc_row(c, Y, y)],
+        lambda p: r.wb_all.at[yc_row(p & (C - 1), Y, p >> log2(C))],
+        r.s_ay,
+        most(r.wb_all),
+        most(r.wb_all),
+    )
+    ex_ay.start()
+
+    r.hf_recv[zq] = jnp.zeros((HD, F), BF16)
+    ex_bhf.wait()
+    hub_mine = r.hf_own[zq] + jnp.sum(r.hf_recv[...].astype(F32), axis=0)
     high = hub_mine.astype(BF16)
     low = (hub_mine - high.astype(F32)).astype(BF16)
     hub_hot_t = (
@@ -635,22 +711,15 @@
     ng_out = local(6, r.ng, r.node_grad)
     ng_out.start()
 
-    ex_az.wait()
-    r.wb_all[yc_row(c, Y, y)] = r.wout[...].reshape(DY, F).astype(BF16)
-    ex_ay = exchange(
-        gyc,
-        lambda p: r.wb_all.at[yc_row(c, Y, y)],
-        lambda p: r.wb_all.at[yc_row(p & (C - 1), Y, p >> log2(C))],
-        r.s_ay,
-        most(r.wb_all),
-        most(r.wb_all),
-    )
-    ex_ay.start()
+
+    ex_xl.wait()
+    lo_out = local(5, r.lo_recv, r.layer_out)
+    lo_out.start()
+
     ex_bc.wait()
     r.bias_grad[...] = r.bias_core[0, 0:1] + r.bias_core[1, 0:1]
     ex_ay.wait()
-    r.wg_all[...] = r.wb_all[...].astype(F32).reshape(C * Y, Z, DZ, F)
-    r.wg_all[yc_row(c, Y, y)] = r.wout[...]
+    r.wg_all[...] = r.wb_all[...].astype(F32)
 
     w_out = local(7, r.wg_all, r.weight_grad)
     w_out.start()
@@ -711,7 +780,9 @@
     D, R = X * F, N // X
     ZC, YCC = Z * CUT, Y * C * CUT
     DY = D // Y
-    DZ = DY // Z
+    RES = Z // 4 if Z >= 8 else Z
+    ZQ = Z // RES
+    DN = DY // RES
 
     at = jnp.arange(NT, dtype=jnp.int32)
     key = jnp.where(at < tile_count[0], tile_dst * SB + tile_src, -1)
@@ -748,7 +819,7 @@
     outputs = dict(
         layer_out=(jax.ShapeDtypeStruct((X, R, F), BF16), hbm),
         node_grad=(jax.ShapeDtypeStruct((N, F), BF16), hbm),
-        weight_grad=(jax.ShapeDtypeStruct((C * Y, Z, DZ, F), F32), hbm),
+        weight_grad=(jax.ShapeDtypeStruct((C * Y, DY, F), F32), hbm),
         bias_grad=(jax.ShapeDtypeStruct((1, F), F32), vm),
     )
     scratch = dict(
@@ -763,7 +834,7 @@
         st1=b(Y * C, ZC, F),
         st2=b(Z, YCC, F),
         halo_z=b(Z, YCC, F),
-        hub=b(Y, Z, C, HD, F),
+        hub=b(Y, ZQ, RES, C, HD, F),
         acc=f(F + 16, N),
         inv=f(8, N),
         selfc=b(R, D),
@@ -778,7 +849,7 @@
         lo_recv=b(X, R, F),
         wv=b(2 * D, F),
         ogv=b(N, F),
-        wg_all=f(C * Y, Z, DZ, F),
+        wg_all=f(C * Y, DY, F),
         wb_all=b(C * Y, DY, F),
         gp=b(R, D),
         gm_send=b(X, R, F),
@@ -794,9 +865,11 @@
         wy_send=b(Y, DY + 16, F),
         wy_recv=b(Y, DY + 16, F),
         wy_own=f(Y, DY, F),
-        wz_send=f(Z, DZ + 8, F),
-        wz_recv=f(Z, DZ + 8, F),
-        wout=f(Z, DZ, F),
+        wn_own=f(RES, DN, F),
+        wn_send=b(RES, DN + 16, F),
+        wn_recv=b(RES, DN + 16, F),
+        wf_all=b(ZQ, DN + 16, F),
+        wa=b(RES, DN, F),
         bias_core=f(C, 8, F),
         hs32=f(C, Y, Z, HD, F),
         hsb=b(C, Y, Z, HD, F),
@@ -804,8 +877,12 @@
         hy_send=b(Y, Z, HD, F),
         hy_recv=b(Y, Z, HD, F),
         hy_own=f(Z, HD, F),
-        hz_send=b(Z, HD, F),
-        hz_recv=b(Z, HD, F),
+        hz_own=f(RES, ZQ, HD, F),
+        hz_send=b(RES, ZQ, HD, F),
+        hz_recv=b(RES, ZQ, HD, F),
+        hf_own=f(ZQ, HD, F),
+        hf_send=b(ZQ, HD, F),
+        hf_recv=b(ZQ, HD, F),
         halo_zb=b(Z, YCC, F),
         rt1=b(Z, YCC, F),
         halo_m=b(Y * C, ZC, F),
@@ -815,7 +892,7 @@
         local_sem=pltpu.SemaphoreType.DMA((8,)),
         s_yc=sem(Y * C),
         s_z=sem(Z),
-        s_hz=sem(Z),
+        s_hz=sem(ZQ),
         s_hy=sem(Y),
         s_hc=sem(Y),
         s_xs=sem(X),
@@ -830,13 +907,16 @@
         s_gc=sem(C),
         s_gx=sem(X),
         s_gy=sem(Y),
-        s_gz=sem(Z),
-        s_az=sem(Z),
+        s_gn=sem(RES),
+        s_gf=sem(ZQ),
+        s_az=sem(RES),
         s_ay=sem(Y * C),
         s_bc=sem(C),
         s_bhc=sem(Y),
         s_bhy=sem(Y),
-        s_bhz=sem(Z),
+        s_bhn=sem(RES),
+        s_bhf=sem(ZQ),
+        s_hn=sem(RES),
         s_rz=sem(Z),
         s_ryc=sem(Y * C),
     )

time: 98.4 us -> 93.6 us (0.951)
  Pallas kernels: 94.8 us -> 90 us
    pallas_call x1, Pallas kernels: 92.6 us -> 87.8 us  [per_device(): pl.pallas_call(functools.partial(kernel, dims, names), out_shape=[shape f...]
where the time goes in v4:
time: 93.6 us; the launch traced here: 93.4 us
  Pallas kernels  90 us (96%)
  other arithmetic  2.05 us (2%)
  between operations  1.29 us (1%)
    pallas_call x1, Pallas kernels, per_device(): pl.pallas_call(functools.partial(kernel, dims, names), out_shape=[shape f...  87.8 us
    pallas_call x1, Pallas kernels, per_device(): pl.pallas_call(copy_kernel, out_shape=[jax.ShapeDtypeStruct(v.shape, v.dt...  2.19 us

profile of v4, /device:TPU:1, one launch (start us, length us, event | category | flops | bytes accessed | tf_op | source)
XLA Modules:
  0.0 93.4 jit_solution(5273362684735893544)
XLA Ops:
  1.3 0.7 compare_select_fusion
  2.0 0.7 select_reduce_fusion.1.refs_7_
  2.7 0.7 select_reduce_fusion.refs_8_
  3.3 87.8 %shard_map.129 = (bf16[4,256,128]{2,1,0:T(8,128)(2,1)}, bf16[1024,128]{1,0:T(8,128)(2,1)}, f32[8,128,128]{2,1,0:T(8,128)}, f32[1,128]{1,0:T(1,128)}) custom-call(bf16[1024,128]{1,0:T(8,128)(2,1)} %refs_0_.1, bf16[1024,128]{1,0:T(8,128)(2,1)} %refs_1_.1, bf16[1024,128]{1,0:T(8,128)(2,1)} %refs_2_.1, bf16[88,128,128]{2,1,0:T(8,128)(2,1)} %refs_3_.1, ...), custom_call_target="tpu_custom_call" | custom-call | tf_op jit(solution)/shard_map/pallas_call | solution.py:924
  91.2 2.2 %shard_map.130 = (bf16[4,256,128]{2,1,0:T(8,128)(2,1)}, bf16[1024,128]{1,0:T(8,128)(2,1)}, f32[8,128,128]{2,1,0:T(8,128)}, f32[1,128]{1,0:T(1,128)}) custom-call(bf16[4,256,128]{2,1,0:T(8,128)(2,1)} %get-tuple-element.12.refs_0_, bf16[1024,128]{1,0:T(8,128)(2,1)} %get-tuple-element.13.refs_1_, f32[8,128,128]{2,1,0:T(8,128)} %get-tuple-element.14.refs_2_, ...), custom_call_target="tpu_custom_call" | custom-call | tf_op jit(solution)/shard_map/pallas_call | solution.py:934

commit v5 on v4

--- a/solution.py
+++ b/solution.py
@@ -467,9 +467,39 @@
         wide = rows.astype(F32)
         return wide[0:8] + wide[8:16]
 
-    cat_self = dot_nt(r.gp[...], r.wfull[0:D, :])
-    for j in range(X):
-        r.gs_send[j] = cat_self[:, j * F : (j + 1) * F].astype(BF16)
+    ex_xg.wait()
+    core_to = Relay(
+        other_core, r.s_bhc, lambda p: r.hsb.at[1 - c, p], lambda p: r.hs_core.at[p]
+    )
+    ex_bhy = exchange(
+        gy, lambda p: r.hy_send.at[p], lambda p: r.hy_recv.at[p],
+        r.s_bhy,
+        most(r.hy_send),
+        most(r.hy_recv),
+    )
+
+    def spread(rows):
+        return dot(r.adj_t[rows, :], r.gm[...].reshape(N, F))
+
+    def back_hub(p):
+        rows = spread(pl.ds(pl.multiple_of(N + HALO + p * PERY, T), PERY)).reshape(Z, C, HD, F)
+        for cc in range(C):
+            r.hs32[cc, p] = rows[:, cc]
+            r.hsb[cc, p] = rows[:, cc].astype(BF16)
+        core_to.start(p)
+
+    def pair_hub(p, own):
+        core_to.copy(p).wait_recv()
+        pair = r.hs32[c, p] + r.hs_core[p].astype(F32)
+        if own:
+            r.hy_own[...] = pair
+        else:
+            r.hy_send[p] = pair.astype(BF16)
+            ex_bhy.start_to(p)
+
+    order = [(y + i) & (Y - 1) for i in range(1, Y)] + [y]
+    back_hub(order[0])
+
     ex_gc.wait()
     for j in range(X):
         cols = slice(j * F, (j + 1) * F)
@@ -486,38 +516,6 @@
     )
     ex_gx.start()
 
-    ex_xg.wait()
-    core_to = Relay(
-        other_core, r.s_bhc, lambda p: r.hsb.at[1 - c, p], lambda p: r.hs_core.at[p]
-    )
-    ex_bhy = exchange(
-        gy, lambda p: r.hy_send.at[p], lambda p: r.hy_recv.at[p],
-        r.s_bhy,
-        most(r.hy_send),
-        most(r.hy_recv),
-    )
-
-    def spread(rows):
-        return dot(r.adj_t[rows, :], r.gm[...].reshape(N, F))
-
-    def back_hub(p):
-        rows = spread(pl.ds(pl.multiple_of(N + HALO + p * PERY, T), PERY)).reshape(Z, C, HD, F)
-        for cc in range(C):
-            r.hs32[cc, p] = rows[:, cc]
-            r.hsb[cc, p] = rows[:, cc].astype(BF16)
-        core_to.start(p)
-
-    def pair_hub(p, own):
-        core_to.copy(p).wait_recv()
-        pair = r.hs32[c, p] + r.hs_core[p].astype(F32)
-        if own:
-            r.hy_own[...] = pair
-        else:
-            r.hy_send[p] = pair.astype(BF16)
-            ex_bhy.start_to(p)
-
-    order = [(y + i) & (Y - 1) for i in range(1, Y)] + [y]
-    back_hub(order[0])
     for i in range(1, Y):
         back_hub(order[i])
         pair_hub(order[i - 1], False)
@@ -555,6 +553,9 @@
     )
     ex_gy.start()
 
+    cat_self = dot_nt(r.gp[...], r.wfull[0:D, :])
+    for j in range(X):
+        r.gs_send[j] = cat_self[:, j * F : (j + 1) * F].astype(BF16)
     ex_xgs = exchange(
         gx, lambda p: r.gs_send.at[p], lambda p: r.gs_recv.at[p],
         r.s_xgs,
@@ -571,8 +572,6 @@
     ex_xl.start()
     r.lo_recv[x] = r.lo_send[:, cols_of(x)]
     r.gs_recv[x] = r.gs_send[x]
-
-    r.total[...] = spread(slice(0, N))
 
     r.wy_recv[y] = jnp.zeros((DY + 16, F), BF16)
     ex_gy.wait()
@@ -595,6 +594,26 @@
     )
     ex_gn.start()
 
+    r.total[...] = spread(slice(0, N))
+
+    r.wn_recv[zr] = jnp.zeros((DN + 16, F), BF16)
+    ex_gn.wait()
+    wsum = r.wn_own[zr]
+    for p in range(RES):
+        wsum = wsum + r.wn_recv[p, 0:DN, :].astype(F32)
+        bsum = bsum + bias_of(r.wn_recv[p, DN : DN + 16, :])
+    r.wf_all[zq, 0:DN, :] = wsum.astype(BF16)
+    r.wf_all[zq, DN : DN + 16, :] = bias_rows(bsum[0:1])
+    ex_gf = exchange(
+        gfar,
+        lambda p: r.wf_all.at[zq],
+        lambda p: r.wf_all.at[p],
+        r.s_gf,
+        most(r.wf_all),
+        most(r.wf_all),
+    )
+    ex_gf.start()
+
     r.hy_recv[y] = jnp.zeros((Z, HD, F), BF16)
     ex_bhy.wait()
     hub_y = r.hy_own[...]
@@ -613,24 +632,6 @@
         most(r.hz_recv),
     )
     ex_bhn.start()
-
-    r.wn_recv[zr] = jnp.zeros((DN + 16, F), BF16)
-    ex_gn.wait()
-    wsum = r.wn_own[zr]
-    for p in range(RES):
-        wsum = wsum + r.wn_recv[p, 0:DN, :].astype(F32)
-        bsum = bsum + bias_of(r.wn_recv[p, DN : DN + 16, :])
-    r.wf_all[zq, 0:DN, :] = wsum.astype(BF16)
-    r.wf_all[zq, DN : DN + 16, :] = bias_rows(bsum[0:1])
-    ex_gf = exchange(
-        gfar,
-        lambda p: r.wf_all.at[zq],
-        lambda p: r.wf_all.at[p],
-        r.s_gf,
-        most(r.wf_all),
-        most(r.wf_all),
-    )
-    ex_gf.start()
 
     ex_rz.wait()
     r.halo_m[...] = (

time: 93.6 us -> 94.4 us (level)
  no operation moved by 1% of the time
where the time goes in v5:
time: 94.4 us; the launch traced here: 94.2 us
  Pallas kernels  90.8 us (96%)
  other arithmetic  2.05 us (2%)
  between operations  1.29 us (1%)
    pallas_call x1, Pallas kernels, per_device(): pl.pallas_call(functools.partial(kernel, dims, names), out_shape=[shape f...  88.6 us
    pallas_call x1, Pallas kernels, per_device(): pl.pallas_call(copy_kernel, out_shape=[jax.ShapeDtypeStruct(v.shape, v.dt...  2.19 us

profile of v5, /device:TPU:1, one launch (start us, length us, event | category | flops | bytes accessed | tf_op | source)
XLA Modules:
  0.0 94.2 jit_solution(18182083528386844188)
XLA Ops:
  1.3 0.7 compare_select_fusion
  2.0 0.7 select_reduce_fusion.1.refs_7_
  2.7 0.7 select_reduce_fusion.refs_8_
  3.3 88.6 %shard_map.129 = (bf16[4,256,128]{2,1,0:T(8,128)(2,1)}, bf16[1024,128]{1,0:T(8,128)(2,1)}, f32[8,128,128]{2,1,0:T(8,128)}, f32[1,128]{1,0:T(1,128)}) custom-call(bf16[1024,128]{1,0:T(8,128)(2,1)} %refs_0_.1, bf16[1024,128]{1,0:T(8,128)(2,1)} %refs_1_.1, bf16[1024,128]{1,0:T(8,128)(2,1)} %refs_2_.1, bf16[88,128,128]{2,1,0:T(8,128)(2,1)} %refs_3_.1, ...), custom_call_target="tpu_custom_call" | custom-call | tf_op jit(solution)/shard_map/pallas_call | solution.py:925
  92.0 2.2 %shard_map.130 = (bf16[4,256,128]{2,1,0:T(8,128)(2,1)}, bf16[1024,128]{1,0:T(8,128)(2,1)}, f32[8,128,128]{2,1,0:T(8,128)}, f32[1,128]{1,0:T(1,128)}) custom-call(bf16[4,256,128]{2,1,0:T(8,128)(2,1)} %get-tuple-element.12.refs_0_, bf16[1024,128]{1,0:T(8,128)(2,1)} %get-tuple-element.13.refs_1_, f32[8,128,128]{2,1,0:T(8,128)} %get-tuple-element.14.refs_2_, ...), custom_call_target="tpu_custom_call" | custom-call | tf_op jit(solution)/shard_map/pallas_call | solution.py:935
